TPU v7x, 32 devices: a whole 2x2x4 slice. The times are simulated.
32 devices in a mesh: ctx: 16 (over z, x, core), head: 2 (over y).
Axes of the slice: x: 2, y: 2, z: 4, core: 2. Of those that a mesh axis runs over, the one named last changes fastest.
Arguments:
- queries: bfloat16 [8192, 4096], P('ctx', 'head'), may hold values from -17 to 17
- key_rows: bfloat16 [8192, 4096], P('ctx', 'head'), may hold values from -17 to 17
- values: bfloat16 [8192, 4096], P('ctx', 'head'), may hold values from -6 to 6
- out_weight: bfloat16 [4096, 4096], P('head', 'ctx'), may hold values from -0.125 to 0.125
- grad_mixed: bfloat16 [8192, 4096], P('ctx'), may hold values from -6 to 6
- link_mask: int32 [64, 5], P('ctx'), may hold values 0 or 1
Outputs:
- mixed_out: bfloat16 [8192, 4096], P('ctx', 'head')
- grad_query: bfloat16 [8192, 4096], P('ctx', 'head')
- grad_key: bfloat16 [8192, 4096], P('ctx', 'head')
- grad_value: bfloat16 [8192, 4096], P('ctx', 'head')
- grad_out_weight: float32 [4096, 4096], P('head', 'ctx')
All inputs are finite; a program needn't handle non-finite values. No bound on the sum of `link_mask` on one device may be relied on, other than what follows from the above.
Results may differ from a plain program's by a relative error of at most 0.02.
Values may be sent and summed in bfloat16 or wider, within the bound.
A program may use at most 384 MiB of HBM per device.

v0:
```python
import math

import jax
import jax.numpy as jnp
from jax import lax
from jax.sharding import PartitionSpec as P

HEAD_DIM = 128
BLK = 128
LEVELS = 5


def passed_along(block, axis, distance):
    devices = range(lax.axis_size(axis))
    route = [(i - distance, i) for i in devices if i - distance in devices]
    return lax.ppermute(block, axis, route)


def for_sending(shard):

    def short(part):
        return part.astype(jnp.bfloat16) if part.dtype == jnp.float32 else part

    return jax.tree.map(short, shard)


def on_device(queries, key_rows, values, out_weight, grad_mixed, link_mask):
    row_count, col_count = queries.shape
    blk_count = row_count // BLK
    head_count = col_count // HEAD_DIM
    score_scale = 1.0 / math.sqrt(HEAD_DIM)
    span_list = [2**depth_index for depth_index in range(LEVELS)]
    offsets = sorted(
        set([1] + [span_size // blk_count for span_size in span_list if span_size >= blk_count])
    )
    shifted = {0: (key_rows, values)}
    for distance in offsets:
        shifted[distance] = passed_along((key_rows, values), "ctx", distance)

    def blocked(array):
        return array.reshape(blk_count, BLK, head_count, HEAD_DIM)

    def level_blocks(member, span_size):
        if span_size < blk_count:
            joined = jnp.concatenate([blocked(shifted[1][member]), blocked(shifted[0][member])], 0)
            return joined[blk_count - span_size : 2 * blk_count - span_size]
        return blocked(shifted[span_size // blk_count][member])

    key_all = jnp.stack(
        [blocked(key_rows)] + [level_blocks(0, span_size) for span_size in span_list], 1
    )
    value_all = jnp.stack(
        [blocked(values)] + [level_blocks(1, span_size) for span_size in span_list], 1
    )
    block_ids = lax.axis_index("ctx") * blk_count + jnp.arange(blk_count, dtype=jnp.int32)
    span_array = jnp.array(span_list, jnp.int32)
    live_link = (block_ids[:, None] - span_array[None, :] >= 0) & (link_mask == 1)
    positions = jnp.arange(BLK)
    causal = positions[:, None] >= positions[None, :]
    self_ok = jnp.broadcast_to(causal[None, None, :, None, :], (blk_count, 1, BLK, 1, BLK))
    level_ok = jnp.broadcast_to(live_link[:, None, None, :, None], (blk_count, 1, BLK, LEVELS, BLK))
    allowed = jnp.concatenate([self_ok, level_ok], 3)
    query_blocks = blocked(queries)
    scores = (
        jnp.einsum("nqhe,nlkhe->nhqlk", query_blocks, key_all, preferred_element_type=jnp.float32)
        * score_scale
    )
    scores = jnp.where(allowed, scores, -jnp.inf)
    top_score = jnp.max(scores, axis=(3, 4), keepdims=True)
    weights = jnp.exp(scores - top_score)
    prob_full = weights / jnp.sum(weights, axis=(3, 4), keepdims=True)
    prob_low = prob_full.astype(jnp.bfloat16)
    attn_blocks = jnp.einsum(
        "nhqlk,nlkhe->nqhe", prob_low, value_all, preferred_element_type=jnp.float32
    ).astype(jnp.bfloat16)
    attended = attn_blocks.reshape(row_count, col_count)
    weight_full = lax.all_gather(out_weight, "ctx", axis=1, tiled=True)
    partial_value = jnp.dot(attended, weight_full, preferred_element_type=jnp.float32)
    mixed_out = lax.psum_scatter(
        partial_value.astype(jnp.bfloat16), "head", scatter_dimension=1, tiled=True
    )
    grad_attn = lax.dot_general(
        grad_mixed, weight_full, (((1,), (1,)), ((), ())), preferred_element_type=jnp.float32
    ).astype(jnp.bfloat16)
    weight_part = lax.dot_general(
        attended, grad_mixed, (((0,), (0,)), ((), ())), preferred_element_type=jnp.float32
    )
    grad_out_weight = lax.psum_scatter(
        weight_part.astype(jnp.bfloat16), "ctx", scatter_dimension=1, tiled=True
    ).astype(jnp.float32)
    grad_blocks = blocked(grad_attn)
    row_delta = jnp.sum(grad_blocks.astype(jnp.float32) * attn_blocks.astype(jnp.float32), axis=3)
    row_delta = jnp.transpose(row_delta, (0, 2, 1))[:, :, :, None, None]
    grad_probs = jnp.einsum(
        "nqhe,nlkhe->nhqlk", grad_blocks, value_all, preferred_element_type=jnp.float32
    )
    grad_scores = (prob_full * (grad_probs - row_delta) * score_scale).astype(jnp.bfloat16)
    grad_query = (
        jnp.einsum("nhqlk,nlkhe->nqhe", grad_scores, key_all, preferred_element_type=jnp.float32)
        .astype(jnp.bfloat16)
        .reshape(row_count, col_count)
    )
    key_terms = jnp.einsum(
        "nhqlk,nqhe->nlkhe", grad_scores, query_blocks, preferred_element_type=jnp.float32
    )
    value_terms = jnp.einsum(
        "nhqlk,nqhe->nlkhe", prob_low, grad_blocks, preferred_element_type=jnp.float32
    )
    zero_blocks = jnp.zeros((blk_count, BLK, head_count, HEAD_DIM), jnp.float32)
    owed = {distance: [zero_blocks, zero_blocks] for distance in offsets}
    owed[0] = [key_terms[:, 0], value_terms[:, 0]]
    for depth_index, span_size in enumerate(span_list):
        for member, term_set in enumerate((key_terms, value_terms)):
            contrib = term_set[:, depth_index + 1]
            if span_size < blk_count:
                placed = jnp.concatenate(
                    [
                        jnp.zeros((blk_count - span_size, BLK, head_count, HEAD_DIM), jnp.float32),
                        contrib,
                        jnp.zeros((span_size, BLK, head_count, HEAD_DIM), jnp.float32),
                    ],
                    0,
                )
                owed[1][member] = owed[1][member] + placed[:blk_count]
                owed[0][member] = owed[0][member] + placed[blk_count:]
            else:
                owed[span_size // blk_count][member] = (
                    owed[span_size // blk_count][member] + contrib
                )
    key_total, value_total = owed[0]
    for distance in offsets:
        arrived = passed_along(
            (for_sending(owed[distance][0]), for_sending(owed[distance][1])), "ctx", -distance
        )
        key_total = key_total + arrived[0]
        value_total = value_total + arrived[1]
    grad_key = key_total.astype(jnp.bfloat16).reshape(row_count, col_count)
    grad_value = value_total.astype(jnp.bfloat16).reshape(row_count, col_count)
    return (mixed_out, grad_query, grad_key, grad_value, grad_out_weight)


def solution(mesh):
    placed = (
        P("ctx", "head"),
        P("ctx", "head"),
        P("ctx", "head"),
        P("head", "ctx"),
        P("ctx", None),
        P("ctx", None),
    )
    return jax.shard_map(
        on_device,
        mesh=mesh,
        in_specs=placed,
        out_specs=(
            P("ctx", "head"),
            P("ctx", "head"),
            P("ctx", "head"),
            P("ctx", "head"),
            P("head", "ctx"),
        ),
        check_vma=False,
    )
```

profile of v0, /device:TPU:15, one launch (start us, length us, event | category | flops | bytes accessed | tf_op | source)
XLA Modules:
  0.0 826.3 jit_solution(8270547063062317537)
XLA Ops:
  7.9 3.7 collective-permute-start
  11.7 3.1 collective-permute-start.1
  14.8 3.2 collective-permute-start.2
  18.0 2.5 collective-permute-start.3
  20.5 1.9 collective-permute-start.4
  22.5 66.1 %collective-permute-done = bf16[512,2048]{1,0:T(8,128)(2,1)S(1)} collective-permute-done((bf16[512,2048]{1,0:T(8,128)(2,1)}, bf16[512,2048]{1,0:T(8,128)(2,1)S(1)}, u32[]{:S(2)}, u32[]{:S(2)}) %collective-permute-start) | collective-permute-done | bytes 2097184 | tf_op jit(solution)/shard_map/ppermute | solution.py:16
  88.6 3.2 collective-permute-start.5
  91.8 2.2 copy.102
  94.0 3.1 copy.35
  97.1 3.5 copy.34
  100.6 3.8 copy.108
  104.4 2.0 copy.114
  106.7 3.9 constant_dynamic-update-slice_fusion.3
  110.6 2.0 copy_dynamic-update-slice_fusion.3
  114.3 2.0 copy.103
  116.3 4.5 copy.33
  120.8 4.5 copy.37
  125.3 53.2 %collective-permute-done.1 = bf16[512,2048]{1,0:T(8,128)(2,1)} collective-permute-done((bf16[512,2048]{1,0:T(8,128)(2,1)}, bf16[512,2048]{1,0:T(8,128)(2,1)}, u32[]{:S(2)}, u32[]{:S(2)}) %collective-permute-start.1) | collective-permute-done | bytes 2097184 | tf_op jit(solution)/shard_map/ppermute | solution.py:16
  178.4 3.6 copy.106
  182.0 4.5 copy.38
  186.5 60.0 %collective-permute-done.2 = bf16[512,2048]{1,0:T(8,128)(2,1)} collective-permute-done((bf16[512,2048]{1,0:T(8,128)(2,1)}, bf16[512,2048]{1,0:T(8,128)(2,1)}, u32[]{:S(2)}, u32[]{:S(2)}) %collective-permute-start.2) | collective-permute-done | bytes 2097184 | tf_op jit(solution)/shard_map/ppermute | solution.py:16
  246.5 3.5 copy.107
  250.0 4.9 copy.39
  255.0 35.8 %collective-permute-done.3 = bf16[512,2048]{1,0:T(8,128)(2,1)} collective-permute-done((bf16[512,2048]{1,0:T(8,128)(2,1)}, bf16[512,2048]{1,0:T(8,128)(2,1)}, u32[]{:S(2)}, u32[]{:S(2)}) %collective-permute-start.3) | collective-permute-done | bytes 2097184 | tf_op jit(solution)/shard_map/ppermute | solution.py:16
  290.8 2.2 copy.109
  293.0 22.8 %collective-permute-done.4 = bf16[512,2048]{1,0:T(8,128)(2,1)} collective-permute-done((bf16[512,2048]{1,0:T(8,128)(2,1)}, bf16[512,2048]{1,0:T(8,128)(2,1)}, u32[]{:S(2)}, u32[]{:S(2)}) %collective-permute-start.4) | collective-permute-done | bytes 2097184 | tf_op jit(solution)/shard_map/ppermute | solution.py:16
  315.8 2.4 copy.112
  318.2 20.7 %collective-permute-done.5 = bf16[512,2048]{1,0:T(8,128)(2,1)} collective-permute-done((bf16[512,2048]{1,0:T(8,128)(2,1)}, bf16[512,2048]{1,0:T(8,128)(2,1)}, u32[]{:S(2)}, u32[]{:S(2)}) %collective-permute-start.5) | collective-permute-done | bytes 2097184 | tf_op jit(solution)/shard_map/ppermute | solution.py:16
  338.9 2.2 copy.113
  357.1 2.0 copy_dynamic-update-slice_fusion.1
  361.0 13.0 %fusion.2 = (f32[4,16,128]{2,1,0:T(8,128)S(1)}, f32[4,16,6,128,128]{4,3,2,1,0:T(8,128)}) fusion(pred[4,128,6,128]{1,3,2,0:T(8,128)(4,1)S(1)} %add_bitcast_fusion, bf16[4,6,128,16,128]{4,2,1,3,0:T(8,128)(2,1)} %copy_dynamic-update-slice_fusion, bf16[4,128,16,128,1]{3,2,1,0,4:T(8,128)(2,1)S(1)} %copy-done.9), kind=kOutput, calls=%fused_computation.5 | convolution fusion | flops 1629478912 | bytes 40271872 | tf_op jit(solution)/shard_map/nqhe,nlkhe->nhqlk/dot_general | solution.py:65
  373.9 10.9 %fusion.1 = f32[4,16,128]{2,1,0:T(8,128)S(1)} fusion(f32[4,16,6,128,128]{4,3,2,1,0:T(8,128)} %get-tuple-element.14, f32[4,16,128]{2,1,0:T(8,128)S(1)} %get-tuple-element.13, pred[4,128,6,128]{1,3,2,0:T(8,128)(4,1)S(1)} %add_bitcast_fusion), kind=kLoop, calls=%fused_computation.4 | loop fusion | flops 25157632 | bytes 25624576 | tf_op jit(solution)/shard_map/reduce_sum | solution.py:71
  384.9 13.8 %fusion.40 = bf16[64,8,16,128]{3,1,2,0:T(8,128)(2,1)S(1)} fusion(bf16[512,4096]{1,0:T(8,128)(2,1)} %param.11, bf16[2048,4096]{1,0:T(8,128)(2,1)} %all-gather.2.cloned.1.call-done), kind=kOutput, calls=%fused_computation.84 | convolution fusion | flops 8590983168 | bytes 23068672 | tf_op jit(solution)/shard_map/dot_general | solution.py:82
  399.4 2.9 copy.52
  402.3 18.1 %multiply_reduce_fusion = (f32[4,128,16]{1,2,0:T(8,128)S(1)}, bf16[4,128,16,128]{1,3,2,0:T(8,128)(2,1)}) fusion(bf16[4,128,16,128]{1,3,2,0:T(8,128)(2,1)} %copy.52, bf16[4,6,128,16,128]{2,4,1,3,0:T(8,128)(2,1)} %constant_dynamic-update-slice_fusion, f32[4,16,128]{2,1,0:T(8,128)S(1)} %fusion.1, f32[4,16,128]{2,1,0:T(8,128)S(1)} %get-tuple-element.13, ...), kind=kOutput, calls=%fused_computation.51 | convolution fusion | flops 1647304704 | bytes 42434560 | tf_op jit(solution)/shard_map/nhqlk,nlkhe->nqhe/dot_general | solution.py:73
  420.3 4.5 copy.49
  424.8 14.9 %convolution_convert_fusion = bf16[2048,4096]{1,0:T(8,128)(2,1)} fusion(bf16[512,4096]{1,0:T(8,128)(2,1)} %param.11, bf16[64,8,16,128]{3,2,1,0:T(8,128)(2,1)} %bitcast.231), kind=kOutput, calls=%fused_computation.6 | convolution fusion | flops 8598323200 | bytes 23068672 | tf_op jit(solution)/shard_map/dot_general | solution.py:85
  441.5 5.1 copy.82
  446.6 14.7 %convolution_convert_fusion.1 = bf16[512,4096]{1,0:T(8,128)(2,1)} fusion(bf16[2048,4096]{1,0:T(8,128)(2,1)} %all-gather.2.cloned.1.call-done, bf16[64,8,16,128]{3,2,1,0:T(8,128)(2,1)S(1)} %bitcast.232), kind=kOutput, calls=%fused_computation.18 | convolution fusion | flops 8592031744 | bytes 23068672 | tf_op jit(solution)/shard_map/dot_general | solution.py:78
  461.3 26.1 %fusion.49 = (bf16[4,6,128,16,128]{2,4,1,3,0:T(8,128)(2,1)}, f32[4,6,128,16,128]{2,4,1,3,0:T(8,128)}) fusion(bf16[4,128,16,128,1]{1,3,4,2,0:T(8,128)(2,1)} %copy.82, f32[4,16,128]{2,1,0:T(8,128)S(1)} %fusion.1, f32[4,16,128]{2,1,0:T(8,128)S(1)} %get-tuple-element.13, f32[4,16,6,128,128]{4,3,2,1,0:T(8,128)} %get-tuple-element.14, ...), kind=kOutput, calls=%fused_computation.98 | convolution fusion | flops 1648361472 | bytes 65470464 | tf_op jit(solution)/shard_map/nhqlk,nqhe->nlkhe/dot_general | solution.py:106
  487.4 22.0 %multiply_convert_fusion = bf16[4,16,128,6,128]{2,4,3,1,0:T(8,128)(2,1)} fusion(f32[4,16,128]{2,1,0:T(8,128)S(1)} %bitcast.233, bf16[4,128,16,128,1]{1,3,4,2,0:T(8,128)(2,1)S(1)} %copy-done.20, bf16[4,6,128,16,128]{2,4,1,3,0:T(8,128)(2,1)} %constant_dynamic-update-slice_fusion, f32[4,16,128]{2,1,0:T(8,128)S(1)} %fusion.1, ...), kind=kOutput, calls=%fused_computation.1 | convolution fusion | flops 1660944384 | bytes 52920320 | tf_op jit(solution)/shard_map/nqhe,nlkhe->nhqlk/dot_general | solution.py:94
  509.5 4.8 slice_bitcast_fusion.9
  516.2 2.1 collective-permute-start.10
  518.3 4.1 slice_bitcast_fusion.1
  522.4 7.2 fusion.23
  529.7 1.9 collective-permute-start.9
  531.6 17.0 %fusion.48 = (bf16[4,6,128,16,128]{4,2,1,3,0:T(8,128)(2,1)}, f32[4,6,128,16,128]{4,2,1,3,0:T(8,128)}) fusion(bf16[4,16,128,6,128]{2,4,3,1,0:T(8,128)(2,1)} %multiply_convert_fusion, bf16[4,128,16,128,1]{3,2,1,0,4:T(8,128)(2,1)S(1)} %copy-done.10), kind=kOutput, calls=%fused_computation.97 | convolution fusion | flops 1616904192 | bytes 52428800 | tf_op jit(solution)/shard_map/nhqlk,nqhe->nlkhe/dot_general | solution.py:103
  548.6 4.1 slice_bitcast_fusion.5
  552.7 7.9 slice_bitcast_fusion.11
  560.7 2.0 collective-permute-start.8
  562.7 2.5 collective-permute-start.7
  565.3 4.5 fusion.20
  569.7 31.9 %collective-permute-done.11 = bf16[4,128,16,128]{1,3,2,0:T(8,128)(2,1)} collective-permute-done((bf16[4,128,16,128]{1,3,2,0:T(8,128)(2,1)}, bf16[4,128,16,128]{1,3,2,0:T(8,128)(2,1)}, u32[]{:S(2)}, u32[]{:S(2)}) %collective-permute-start.11) | collective-permute-done | bytes 2097184 | tf_op jit(solution)/shard_map/ppermute | solution.py:16
  603.6 7.7 fusion.44
  611.2 3.4 copy.56
  616.6 24.7 %collective-permute-done.10 = bf16[4,128,16,128]{1,3,2,0:T(8,128)(2,1)} collective-permute-done((bf16[4,128,16,128]{1,3,2,0:T(8,128)(2,1)}, bf16[4,128,16,128]{1,3,2,0:T(8,128)(2,1)}, u32[]{:S(2)}, u32[]{:S(2)}) %collective-permute-start.10) | collective-permute-done | bytes 2097184 | tf_op jit(solution)/shard_map/ppermute | solution.py:16
  641.3 34.6 %collective-permute-done.9 = bf16[4,128,16,128]{1,3,2,0:T(8,128)(2,1)} collective-permute-done((bf16[4,128,16,128]{1,3,2,0:T(8,128)(2,1)}, bf16[4,128,16,128]{1,3,2,0:T(8,128)(2,1)}, u32[]{:S(2)}, u32[]{:S(2)}) %collective-permute-start.9) | collective-permute-done | bytes 2097184 | tf_op jit(solution)/shard_map/ppermute | solution.py:16
  676.0 5.9 fusion.17
  681.9 2.9 copy.71
  684.8 80.4 %collective-permute-done.7 = bf16[4,128,16,128]{3,1,2,0:T(8,128)(2,1)} collective-permute-done((bf16[4,128,16,128]{3,1,2,0:T(8,128)(2,1)}, bf16[4,128,16,128]{3,1,2,0:T(8,128)(2,1)}, u32[]{:S(2)}, u32[]{:S(2)}) %collective-permute-start.7) | collective-permute-done | bytes 2097184 | tf_op jit(solution)/shard_map/ppermute | solution.py:16
  765.1 39.5 %collective-permute-done.6 = bf16[4,128,16,128]{3,1,2,0:T(8,128)(2,1)} collective-permute-done((bf16[4,128,16,128]{3,1,2,0:T(8,128)(2,1)}, bf16[4,128,16,128]{3,1,2,0:T(8,128)(2,1)}, u32[]{:S(2)}, u32[]{:S(2)}) %collective-permute-start.6) | collective-permute-done | bytes 2097184 | tf_op jit(solution)/shard_map/ppermute | solution.py:16
  804.7 6.4 fusion.11
  812.8 4.1 copy_bitcast_fusion
  816.9 2.7 convert_element_type.107
  (87 shorter events, 30.4 us)
Async XLA Ops:
  7.2 377.7 %all-gather.2.cloned.1.call-start = ((), (), s32[]{:S(2)}) async-start(), calls=%async_computation.2 | async-start | bytes 17825792 | tf_op jit(solution)/shard_map/all_gather | solution.py:77
  7.9 809.0 %reduce-scatter.5.cloned.1.call-start = ((), (), s32[]{:S(2)}) async-start(), calls=%async_computation.4 | async-start | bytes 17825792 | tf_op jit(solution)/shard_map/reduce_scatter | solution.py:88
  7.9 80.6 %collective-permute-start = (bf16[512,2048]{1,0:T(8,128)(2,1)}, bf16[512,2048]{1,0:T(8,128)(2,1)S(1)}, u32[]{:S(2)}, u32[]{:S(2)}) collective-permute-start(bf16[512,2048]{1,0:T(8,128)(2,1)} %param.9), channel_id=1, source_target_pairs={{0,2},{2,4},{4,6},{6,8},{8,10},{10,12},{12,14},{14,16},{16,18},{18... | collective-permute-start | bytes 6291464 | tf_op jit(solution)/shard_map/ppermute | solution.py:16
  11.7 166.8 %collective-permute-start.1 = (bf16[512,2048]{1,0:T(8,128)(2,1)}, bf16[512,2048]{1,0:T(8,128)(2,1)}, u32[]{:S(2)}, u32[]{:S(2)}) collective-permute-start(bf16[512,2048]{1,0:T(8,128)(2,1)} %param.9), channel_id=1, source_target_pairs={{0,4},{2,6},{4,8},{6,10},{8,12},{10,14},{12,16},{14,18},{16,20},{1... | collective-permute-start | bytes 6291464 | tf_op jit(solution)/shard_map/ppermute | solution.py:16
  14.8 231.7 %collective-permute-start.2 = (bf16[512,2048]{1,0:T(8,128)(2,1)}, bf16[512,2048]{1,0:T(8,128)(2,1)}, u32[]{:S(2)}, u32[]{:S(2)}) collective-permute-start(bf16[512,2048]{1,0:T(8,128)(2,1)} %param.9), channel_id=1, source_target_pairs={{0,8},{2,10},{4,12},{6,14},{8,16},{10,18},{12,20},{14,22},{16,24},... | collective-permute-start | bytes 6291464 | tf_op jit(solution)/shard_map/ppermute | solution.py:16
  18.0 272.8 %collective-permute-start.3 = (bf16[512,2048]{1,0:T(8,128)(2,1)}, bf16[512,2048]{1,0:T(8,128)(2,1)}, u32[]{:S(2)}, u32[]{:S(2)}) collective-permute-start(bf16[512,2048]{1,0:T(8,128)(2,1)} %param.8), channel_id=1, source_target_pairs={{0,2},{2,4},{4,6},{6,8},{8,10},{10,12},{12,14},{14,16},{16,18},{18... | collective-permute-start | bytes 6291464 | tf_op jit(solution)/shard_map/ppermute | solution.py:16
  20.5 295.3 %collective-permute-start.4 = (bf16[512,2048]{1,0:T(8,128)(2,1)}, bf16[512,2048]{1,0:T(8,128)(2,1)}, u32[]{:S(2)}, u32[]{:S(2)}) collective-permute-start(bf16[512,2048]{1,0:T(8,128)(2,1)} %param.8), channel_id=1, source_target_pairs={{0,4},{2,6},{4,8},{6,10},{8,12},{10,14},{12,16},{14,18},{16,20},{1... | collective-permute-start | bytes 6291464 | tf_op jit(solution)/shard_map/ppermute | solution.py:16
  88.6 3.2 copy-start.17
  88.6 250.4 %collective-permute-start.5 = (bf16[512,2048]{1,0:T(8,128)(2,1)}, bf16[512,2048]{1,0:T(8,128)(2,1)}, u32[]{:S(2)}, u32[]{:S(2)}) collective-permute-start(bf16[512,2048]{1,0:T(8,128)(2,1)} %param.8), channel_id=1, source_target_pairs={{0,8},{2,10},{4,12},{6,14},{8,16},{10,18},{12,20},{14,22},{16,24},... | collective-permute-start | bytes 6291464 | tf_op jit(solution)/shard_map/ppermute | solution.py:16
  94.0 3.1 copy-start.8
  100.6 3.8 copy-start.16
  100.6 5.8 copy-start.21
  100.6 5.8 copy-start.22
  106.4 4.2 copy-start.6
  106.7 5.9 copy-start.14
  110.6 3.7 copy-start.18
  315.8 25.3 %copy-start.5 = (bf16[4,128,16,128]{1,3,2,0:T(8,128)(2,1)S(1)}, bf16[4,128,16,128]{1,3,2,0:T(8,128)(2,1)}, u32[]{:S(2)}) copy-start(bf16[4,128,16,128]{1,3,2,0:T(8,128)(2,1)} %copy.33) | copy-start | bytes 6291460
  342.9 2.2 copy-start.11
  342.9 4.0 copy-start.12
  345.1 3.5 copy-start.13
  348.6 2.3 copy-start.7
  357.1 3.9 copy-start.9
  439.8 379.8 %reduce-scatter.3.cloned.1.call-start = ((), (), s32[]{:S(2)}) async-start(), calls=%async_computation.3 | async-start | bytes 6291456 | tf_op jit(solution)/shard_map/reduce_scatter | solution.py:79
  441.5 5.1 copy-start.19
  461.3 26.1 %copy-start.20 = (bf16[4,128,16,128,1]{1,3,4,2,0:T(8,128)(2,1)S(1)}, bf16[4,128,16,128,1]{1,3,4,2,0:T(8,128)(2,1)}, u32[]{:S(2)}) copy-start(bf16[4,128,16,128,1]{1,3,4,2,0:T(8,128)(2,1)} %copy.82) | copy-start | bytes 6291460
  514.3 87.3 %collective-permute-start.11 = (bf16[4,128,16,128]{1,3,2,0:T(8,128)(2,1)}, bf16[4,128,16,128]{1,3,2,0:T(8,128)(2,1)}, u32[]{:S(2)}, u32[]{:S(2)}) collective-permute-start(bf16[4,128,16,128]{1,3,2,0:T(8,128)(2,1)} %get-tuple-element.10), channel_id=1, source_target_pairs={{8,0},{10,2},{12,4},{14,6},{16,8},{18,10},{20,12},{22,14},{24,16},... | collective-permute-start | bytes 6291464 | tf_op jit(solution)/shard_map/ppermute | solution.py:16
  516.2 125.1 %collective-permute-start.10 = (bf16[4,128,16,128]{1,3,2,0:T(8,128)(2,1)}, bf16[4,128,16,128]{1,3,2,0:T(8,128)(2,1)}, u32[]{:S(2)}, u32[]{:S(2)}) collective-permute-start(bf16[4,128,16,128]{1,3,2,0:T(8,128)(2,1)} %get-tuple-element.9), channel_id=1, source_target_pairs={{4,0},{6,2},{8,4},{10,6},{12,8},{14,10},{16,12},{18,14},{20,16},{2... | collective-permute-start | bytes 6291464 | tf_op jit(solution)/shard_map/ppermute | solution.py:16
  522.4 7.3 copy-start.2
  522.4 7.3 copy-start.4
  522.4 9.2 %copy-start.10 = (bf16[4,128,16,128,1]{3,2,1,0,4:T(8,128)(2,1)S(1)}, bf16[4,128,16,128,1]{3,2,1,0,4:T(8,128)(2,1)}, u32[]{:S(2)}) copy-start(bf16[4,128,16,128,1]{3,2,1,0,4:T(8,128)(2,1)} %bitcast_bitcast_fusion) | copy-start | bytes 6291460
  529.7 146.3 %collective-permute-start.9 = (bf16[4,128,16,128]{1,3,2,0:T(8,128)(2,1)}, bf16[4,128,16,128]{1,3,2,0:T(8,128)(2,1)}, u32[]{:S(2)}, u32[]{:S(2)}) collective-permute-start(bf16[4,128,16,128]{1,3,2,0:T(8,128)(2,1)} %fusion.23), channel_id=1, source_target_pairs={{2,0},{4,2},{6,4},{8,6},{10,8},{12,10},{14,12},{16,14},{18,16},{20... | collective-permute-start | bytes 6291464 | tf_op jit(solution)/shard_map/ppermute | solution.py:16
  552.7 12.5 %copy-start = (f32[4,128,16,128]{3,1,2,0:T(8,128)}, f32[4,128,16,128]{3,1,2,0:T(8,128)S(1)}, u32[]{:S(2)}) copy-start(f32[4,128,16,128]{3,1,2,0:T(8,128)S(1)} %get-tuple-element.7) | copy-start | bytes 12582916
  552.7 12.5 %copy-start.1 = (f32[4,128,16,128]{3,1,2,0:T(8,128)}, f32[4,128,16,128]{3,1,2,0:T(8,128)S(1)}, u32[]{:S(2)}) copy-start(f32[4,128,16,128]{3,1,2,0:T(8,128)S(1)} %get-tuple-element.8) | copy-start | bytes 12582916
  552.7 50.8 %slice-start = ((s8[12582912]{0:T(1024)(128)(4,1)}), s8[4194304]{0:T(1024)(128)(4,1)S(1)}, s32[]{:S(2)}) async-start(s8[12582912]{0:T(1024)(128)(4,1)} %bitcast.206), calls=%async_computation.5 | async-start | bytes 8388608
  552.7 50.8 %slice-start.1 = ((s8[12582912]{0:T(1024)(128)(4,1)}), s8[4194304]{0:T(1024)(128)(4,1)S(1)}, s32[]{:S(2)}) async-start(s8[12582912]{0:T(1024)(128)(4,1)} %bitcast.206), calls=%async_computation.6 | async-start | bytes 8388608
  560.7 124.1 %collective-permute-start.8 = (bf16[4,128,16,128]{3,1,2,0:T(8,128)(2,1)}, bf16[4,128,16,128]{3,1,2,0:T(8,128)(2,1)}, u32[]{:S(2)}, u32[]{:S(2)}) collective-permute-start(bf16[4,128,16,128]{3,1,2,0:T(8,128)(2,1)} %get-tuple-element.12), channel_id=1, source_target_pairs={{8,0},{10,2},{12,4},{14,6},{16,8},{18,10},{20,12},{22,14},{24,16},... | collective-permute-start | bytes 6291464 | tf_op jit(solution)/shard_map/ppermute | solution.py:16
  562.7 202.4 %collective-permute-start.7 = (bf16[4,128,16,128]{3,1,2,0:T(8,128)(2,1)}, bf16[4,128,16,128]{3,1,2,0:T(8,128)(2,1)}, u32[]{:S(2)}, u32[]{:S(2)}) collective-permute-start(bf16[4,128,16,128]{3,1,2,0:T(8,128)(2,1)} %get-tuple-element.11), channel_id=1, source_target_pairs={{4,0},{6,2},{8,4},{10,6},{12,8},{14,10},{16,12},{18,14},{20,16},{2... | collective-permute-start | bytes 6291464 | tf_op jit(solution)/shard_map/ppermute | solution.py:16
  565.2 38.3 %slice-start.2 = ((s8[12582912]{0:T(1024)(128)(4,1)}), s8[4194304]{0:T(1024)(128)(4,1)S(1)}, s32[]{:S(2)}) async-start(s8[12582912]{0:T(1024)(128)(4,1)} %bitcast.206), calls=%async_computation.7 | async-start | bytes 8388608
  601.6 203.0 %collective-permute-start.6 = (bf16[4,128,16,128]{3,1,2,0:T(8,128)(2,1)}, bf16[4,128,16,128]{3,1,2,0:T(8,128)(2,1)}, u32[]{:S(2)}, u32[]{:S(2)}) collective-permute-start(bf16[4,128,16,128]{3,1,2,0:T(8,128)(2,1)} %fusion.20), channel_id=1, source_target_pairs={{2,0},{4,2},{6,4},{8,6},{10,8},{12,10},{14,12},{16,14},{18,16},{20... | collective-permute-start | bytes 6291464 | tf_op jit(solution)/shard_map/ppermute | solution.py:16
  614.7 61.3 %copy-start.3 = (f32[4,128,16,128]{1,3,2,0:T(8,128)S(1)}, f32[4,128,16,128]{1,3,2,0:T(8,128)}, u32[]{:S(2)}) copy-start(f32[4,128,16,128]{1,3,2,0:T(8,128)} %copy-done.2) | copy-start | bytes 12582916
  811.1 1.7 copy-start.15
Sparse Core Ops, SparseCore 0:
  10.2 227.0 all-gather.1
  439.9 282.2 reduce-scatter.4
  725.1 86.6 reduce-scatter.2
where the time goes:
time: 833 us; the launch traced here: 826 us
  waiting for transfers between devices  471 us (57%)
  matrix products  147 us (18%)
  local copies, waits for them, and re-layouts  123 us (15%)
  other arithmetic  41.3 us (5%)
  starting transfers between devices  30.2 us (4%)
  between operations  14.4 us (2%)
    ppermute x12, waiting for transfers between devices, passed_along(): return lax.ppermute(block, axis, route)  470 us
    unnamed x72, local copies, waits for them, and re-layouts  44.4 us
    ppermute x12, starting transfers between devices, passed_along(): return lax.ppermute(block, axis, route)  30 us
    dot_general x1, matrix products, on_device(): jnp.einsum('nhqlk,nqhe->nlkhe', prob_low, grad_blocks, preferred_element_...  26.1 us
    dot_general x1, matrix products, on_device(): jnp.einsum('nqhe,nlkhe->nhqlk', grad_blocks, value_all, preferred_element...  22 us
    reshape x6, local copies, waits for them, and re-layouts, blocked(): return array.reshape(blk_count, BLK, head_count, HEAD_DIM)  19.4 us
    another operation x5, local copies, waits for them, and re-layouts, on_device(): jnp.stack([blocked(values)] + [level_blocks(1, span_size) for span_size i...  18.8 us
    dot_general x1, matrix products, on_device(): jnp.einsum('nhqlk,nlkhe->nqhe', prob_low, value_all, preferred_element_ty...  18.1 us
  transfers between devices with their start and end apart: 15, of which 11 were waited for; matrix products, arithmetic and copies ran while one was open for 31% of the time, Pallas kernels for 0%

commit v1 on v0

v1 whole, which is shorter than its diff:
```python
import functools
import math

import jax
import jax.numpy as jnp
from jax import lax
from jax.experimental import pallas as pl
from jax.experimental.pallas import tpu as pltpu
from jax.sharding import PartitionSpec as P

HEAD_DIM = 128
BLK = 128
LEVELS = 5
PAIR = 2
DEAD = -1e30


def passed_along(block, axis, distance):
    devices = range(lax.axis_size(axis))
    route = [(i - distance, i) for i in devices if i - distance in devices]
    return lax.ppermute(block, axis, route)


def reach(block, span, count):
    if span >= count:
        return span // count, block
    if 0 <= block + span < count:
        return 0, block + span
    return 1, (block + span) % count


def reach_back(block, span, count):
    if span >= count:
        return span // count, block
    if block - span >= 0:
        return 0, block - span
    return 1, block - span + count


def rows_of(block):
    return slice(block * BLK, (block + 1) * BLK)


def dot_nt(a, b):
    return lax.dot_general(a, b, (((1,), (1,)), ((), ())), preferred_element_type=jnp.float32)


def dot_nn(a, b):
    return lax.dot_general(a, b, (((1,), (0,)), ((), ())), preferred_element_type=jnp.float32)


def as_row(column):
    return jnp.broadcast_to(column, (BLK, BLK)).T[:1]


def query_side(offsets, scale, live_ref, q_ref, g_ref, *refs):
    sources = [0] + offsets
    keys = {d: refs[2 * n] for n, d in enumerate(sources)}
    vals = {d: refs[2 * n + 1] for n, d in enumerate(sources)}
    att_ref, dq_ref, stat_ref = refs[2 * len(sources):]
    count = q_ref.shape[0] // BLK
    causal = lax.broadcasted_iota(jnp.int32, (BLK, BLK), 0) >= lax.broadcasted_iota(
        jnp.int32, (BLK, BLK), 1
    )
    for h in range(PAIR):
        cols = slice(h * HEAD_DIM, (h + 1) * HEAD_DIM)
        for b in range(count):
            rows = rows_of(b)
            q = q_ref[rows, cols]
            g = g_ref[rows, cols]
            where = [(0, b)] + [reach_back(b, 2**l, count) for l in range(LEVELS)]
            kc = jnp.concatenate([keys[d][rows_of(c), cols] for d, c in where], 0)
            vc = jnp.concatenate([vals[d][rows_of(c), cols] for d, c in where], 0)
            s = dot_nt(q, kc) * scale
            parts = [jnp.where(causal, s[:, :BLK], DEAD)]
            for l in range(LEVELS):
                part = s[:, (l + 1) * BLK : (l + 2) * BLK]
                parts.append(jnp.where(live_ref[b, l] > 0, part, DEAD))
            s = jnp.concatenate(parts, 1)
            top = jnp.max(s, axis=1, keepdims=True)
            w = jnp.exp(s - top)
            total = jnp.sum(w, axis=1, keepdims=True)
            prob = w * (1.0 / total)
            att = dot_nn(prob.astype(jnp.bfloat16), vc).astype(jnp.bfloat16)
            att_ref[rows, cols] = att
            delta = jnp.sum(
                g.astype(jnp.float32) * att.astype(jnp.float32), axis=1, keepdims=True
            )
            ds = (prob * ((dot_nt(g, vc) - delta) * scale)).astype(jnp.bfloat16)
            dq_ref[rows, cols] = dot_nn(ds, kc).astype(jnp.bfloat16)
            stat_ref[0, h : h + 1, rows] = as_row(top + jnp.log(total))
            stat_ref[0, PAIR + h : PAIR + h + 1, rows] = as_row(delta)


def key_side(offsets, scale, link_ref, k_ref, v_ref, *refs):
    sources = [0] + offsets
    quer = {d: refs[3 * n] for n, d in enumerate(sources)}
    grad = {d: refs[3 * n + 1] for n, d in enumerate(sources)}
    stat = {d: refs[3 * n + 2] for n, d in enumerate(sources)}
    at = {d: n for n, d in enumerate(sources)}
    dk_ref, dv_ref = refs[3 * len(sources):]
    count = k_ref.shape[0] // BLK
    causal = lax.broadcasted_iota(jnp.int32, (BLK, BLK), 0) <= lax.broadcasted_iota(
        jnp.int32, (BLK, BLK), 1
    )
    for h in range(PAIR):
        cols = slice(h * HEAD_DIM, (h + 1) * HEAD_DIM)
        for b in range(count):
            rows = rows_of(b)
            k = k_ref[rows, cols]
            v = v_ref[rows, cols]
            where = [(0, b)] + [reach(b, 2**l, count) for l in range(LEVELS)]
            qc = jnp.concatenate([quer[d][rows_of(c), cols] for d, c in where], 0)
            gc = jnp.concatenate([grad[d][rows_of(c), cols] for d, c in where], 0)
            lse = jnp.concatenate([stat[d][0, h : h + 1, rows_of(c)] for d, c in where], 1)
            delta = jnp.concatenate(
                [stat[d][0, PAIR + h : PAIR + h + 1, rows_of(c)] for d, c in where], 1
            )
            s = dot_nt(k, qc) * scale - lse
            parts = [jnp.where(causal, s[:, :BLK], DEAD)]
            for l in range(LEVELS):
                d, c = where[l + 1]
                part = s[:, (l + 1) * BLK : (l + 2) * BLK]
                parts.append(jnp.where(link_ref[at[d] * count + c, l] == 1, part, DEAD))
            prob = jnp.exp(jnp.concatenate(parts, 1))
            dv_ref[rows, cols] = dot_nn(prob.astype(jnp.bfloat16), gc).astype(jnp.bfloat16)
            ds = (prob * ((dot_nt(v, gc) - delta) * scale)).astype(jnp.bfloat16)
            dk_ref[rows, cols] = dot_nn(ds, qc).astype(jnp.bfloat16)


def on_device(queries, key_rows, values, out_weight, grad_mixed, link_mask):
    row_count, col_count = queries.shape
    blk_count = row_count // BLK
    head_count = col_count // HEAD_DIM
    steps = head_count // PAIR
    score_scale = 1.0 / math.sqrt(HEAD_DIM)
    span_list = [2**depth_index for depth_index in range(LEVELS)]
    offsets = sorted(
        set([1] + [span_size // blk_count for span_size in span_list if span_size >= blk_count])
    )
    block_ids = lax.axis_index("ctx") * blk_count + jnp.arange(blk_count, dtype=jnp.int32)
    span_array = jnp.array(span_list, jnp.int32)
    live = ((block_ids[:, None] - span_array[None, :] >= 0) & (link_mask == 1)).astype(jnp.int32)

    weight_full = lax.all_gather(out_weight, "ctx", axis=1, tiled=True)
    kv = [key_rows, values]
    for distance in offsets:
        kv += list(passed_along((key_rows, values), "ctx", distance))
    later_queries = [passed_along(queries, "ctx", -distance) for distance in offsets]
    links = jnp.concatenate(
        [link_mask] + [passed_along(link_mask, "ctx", -distance) for distance in offsets], 0
    )

    grad_attn = lax.dot_general(
        grad_mixed, weight_full, (((1,), (1,)), ((), ())), preferred_element_type=jnp.float32
    ).astype(jnp.bfloat16)
    later_grads = [passed_along(grad_attn, "ctx", -distance) for distance in offsets]

    wide = pl.BlockSpec((row_count, PAIR * HEAD_DIM), lambda i: (0, i))
    narrow = pl.BlockSpec((1, 2 * PAIR, row_count), lambda i: (i, 0, 0))
    scalars = pl.BlockSpec(memory_space=pltpu.SMEM)
    like_rows = jax.ShapeDtypeStruct((row_count, col_count), jnp.bfloat16)
    like_stat = jax.ShapeDtypeStruct((steps, 2 * PAIR, row_count), jnp.float32)
    tiles = blk_count * head_count * (LEVELS + 1)
    cost = pl.CostEstimate(
        flops=4 * 2 * tiles * BLK * BLK * HEAD_DIM * 4,
        bytes_accessed=12 * row_count * col_count * 2,
        transcendentals=tiles * BLK * BLK,
    )
    params = pltpu.CompilerParams(vmem_limit_bytes=48 * 1024 * 1024)
    attended, grad_query, stats = pl.pallas_call(
        functools.partial(query_side, offsets, score_scale),
        grid=(steps,),
        in_specs=[scalars] + [wide] * (2 + len(kv)),
        out_specs=[wide, wide, narrow],
        out_shape=[like_rows, like_rows, like_stat],
        compiler_params=params,
        cost_estimate=cost,
        name="query_side",
    )(live, queries, grad_attn, *kv)
    later_stats = [passed_along(stats, "ctx", -distance) for distance in offsets]

    weight_part = lax.dot_general(
        attended, grad_mixed, (((0,), (0,)), ((), ())), preferred_element_type=jnp.float32
    )
    grad_out_weight = lax.psum_scatter(
        weight_part.astype(jnp.bfloat16), "ctx", scatter_dimension=1, tiled=True
    ).astype(jnp.float32)
    partial_value = jnp.dot(attended, weight_full, preferred_element_type=jnp.float32)
    mixed_out = lax.psum_scatter(
        partial_value.astype(jnp.bfloat16), "head", scatter_dimension=1, tiled=True
    )

    triples = [queries, grad_attn, stats]
    for n in range(len(offsets)):
        triples += [later_queries[n], later_grads[n], later_stats[n]]
    grad_key, grad_value = pl.pallas_call(
        functools.partial(key_side, offsets, score_scale),
        grid=(steps,),
        in_specs=[scalars, wide, wide] + [wide, wide, narrow] * (1 + len(offsets)),
        out_specs=[wide, wide],
        out_shape=[like_rows, like_rows],
        compiler_params=params,
        cost_estimate=cost,
        name="key_side",
    )(links, key_rows, values, *triples)
    return (mixed_out, grad_query, grad_key, grad_value, grad_out_weight)


def solution(mesh):
    placed = (
        P("ctx", "head"),
        P("ctx", "head"),
        P("ctx", "head"),
        P("head", "ctx"),
        P("ctx", None),
        P("ctx", None),
    )
    return jax.shard_map(
        on_device,
        mesh=mesh,
        in_specs=placed,
        out_specs=(
            P("ctx", "head"),
            P("ctx", "head"),
            P("ctx", "head"),
            P("ctx", "head"),
            P("head", "ctx"),
        ),
        check_vma=False,
    )
```

time: 833 us -> 806 us (0.968)
  waiting for transfers between devices: 471 us -> 589 us
  local copies, waits for them, and re-layouts: 123 us -> 6.55 us
  matrix products: 147 us -> 41.6 us
  Pallas kernels: 0 us -> 77 us
  starting transfers between devices: 30.2 us -> 73.4 us
  other arithmetic: 41.3 us -> 3.48 us
    all_gather x1, waiting for transfers between devices: 0.02 us -> 145 us  [on_device(): weight_full = lax.all_gather(out_weight, 'ctx', axis=1, tiled=True)]
    dot_general x6 -> x0, matrix products: 104 us -> none  [the longest x1 26.1 us: on_device(): jnp.einsum('nhqlk,nqhe->nlkhe', prob_low, grad_blocks, preferred_element_...]
    pallas_call x0 -> x2, Pallas kernels: none -> 77 us  [the longest x1 47.2 us: on_device(): pl.pallas_call(functools.partial(query_side, offsets, score_scale), grid=...]
    ppermute x12 -> x18, starting transfers between devices: 30 us -> 73.3 us  [passed_along(): return lax.ppermute(block, axis, route)]
    unnamed x72 -> x22, local copies, waits for them, and re-layouts: 44.4 us -> 6.55 us
    ppermute x12 -> x18, waiting for transfers between devices: 470 us -> 443 us  [passed_along(): return lax.ppermute(block, axis, route)]
    convert_element_type x6 -> x0, local copies, waits for them, and re-layouts: 24.9 us -> none  [the longest x2 12.8 us: short(): return part.astype(jnp.bfloat16) if part.dtype == jnp.float32 else part]
    reshape x7 -> x0, local copies, waits for them, and re-layouts: 23.5 us -> none  [the longest x6 19.4 us: blocked(): return array.reshape(blk_count, BLK, head_count, HEAD_DIM)]
  transfers between devices with their start and end apart: 15 -> 21, of which waited for: 11 -> 10; matrix products, arithmetic and copies ran while one was open for 31% -> 4% of each run, Pallas kernels for 0% -> 4%
where the time goes in v1:
time: 806 us; the launch traced here: 805 us
  waiting for transfers between devices  589 us (73%)
  Pallas kernels  77 us (10%)
  starting transfers between devices  73.4 us (9%)
  matrix products  41.6 us (5%)
  between operations  14 us (2%)
    ppermute x18, waiting for transfers between devices, passed_along(): return lax.ppermute(block, axis, route)  443 us
    all_gather x1, waiting for transfers between devices, on_device(): weight_full = lax.all_gather(out_weight, 'ctx', axis=1, tiled=True)  145 us
    ppermute x18, starting transfers between devices, passed_along(): return lax.ppermute(block, axis, route)  73.3 us
    pallas_call x1, Pallas kernels, on_device(): pl.pallas_call(functools.partial(query_side, offsets, score_scale), grid=...  47.2 us
    pallas_call x1, Pallas kernels, on_device(): pl.pallas_call(functools.partial(key_side, offsets, score_scale), grid=(s...  29.8 us
  transfers between devices with their start and end apart: 21, of which 10 were waited for; matrix products, arithmetic and copies ran while one was open for 4% of the time, Pallas kernels for 4%

profile of v1, /device:TPU:15, one launch (start us, length us, event | category | flops | bytes accessed | tf_op | source)
XLA Modules:
  0.0 804.9 jit_solution(14953964326817725453)
XLA Ops:
  7.2 0.0 all-gather.2.cloned.1.call-start
  7.2 0.7 all-gather.2.cloned.1.call-update
  7.9 0.0 reduce-scatter.5.cloned.1.call-start
  7.9 3.7 collective-permute-start
  11.7 3.1 collective-permute-start.2
  14.8 2.2 collective-permute-start.1
  17.0 3.2 collective-permute-start.3
  20.2 2.0 collective-permute-start.4
  22.2 0.8 fusion.1.live_ref
  23.0 65.6 %collective-permute-done.refs_2_ = bf16[512,2048]{1,0:T(8,128)(2,1)} collective-permute-done((bf16[512,2048]{1,0:T(8,128)(2,1)}, bf16[512,2048]{1,0:T(8,128)(2,1)}, u32[]{:S(2)}, u32[]{:S(2)}) %collective-permute-start) | collective-permute-done | bytes 2097184 | tf_op jit(solution)/shard_map/ppermute | solution.py:21
  88.6 3.2 collective-permute-start.5
  91.8 145.5 %all-gather.2.cloned.1.call-done = bf16[2048,4096]{1,0:T(8,128)(2,1)} async-done(((bf16[2048,256]{1,0:T(8,128)(2,1)}), bf16[2048,4096]{1,0:T(8,128)(2,1)}) %all-gather.2.cloned.1.call-update) | async-done | bytes 16777232 | tf_op jit(solution)/shard_map/all_gather | solution.py:145
  237.3 14.6 %convolution_convert_fusion.2.g_ref.refs_1_ = bf16[512,2048]{1,0:T(8,128)(2,1)} fusion(bf16[512,4096]{1,0:T(8,128)(2,1)} %param.11, bf16[2048,4096]{1,0:T(8,128)(2,1)} %all-gather.2.cloned.1.call-done), kind=kOutput, calls=%fused_computation.2 | convolution fusion | flops 8590983168 | bytes 23068672 | tf_op jit(solution)/shard_map/dot_general | solution.py:154
  251.9 0.0 collective-permute-done.1.refs_3_
  251.9 0.0 collective-permute-done.2.refs_4_
  251.9 38.9 %collective-permute-done.3.refs_5_ = bf16[512,2048]{1,0:T(8,128)(2,1)} collective-permute-done((bf16[512,2048]{1,0:T(8,128)(2,1)}, bf16[512,2048]{1,0:T(8,128)(2,1)}, u32[]{:S(2)}, u32[]{:S(2)}) %collective-permute-start.3) | collective-permute-done | bytes 2097184 | tf_op jit(solution)/shard_map/ppermute | solution.py:21
  290.8 25.7 %collective-permute-done.4.refs_6_ = bf16[512,2048]{1,0:T(8,128)(2,1)} collective-permute-done((bf16[512,2048]{1,0:T(8,128)(2,1)}, bf16[512,2048]{1,0:T(8,128)(2,1)}, u32[]{:S(2)}, u32[]{:S(2)}) %collective-permute-start.4) | collective-permute-done | bytes 2097184 | tf_op jit(solution)/shard_map/ppermute | solution.py:21
  316.5 22.5 %collective-permute-done.5.refs_7_ = bf16[512,2048]{1,0:T(8,128)(2,1)} collective-permute-done((bf16[512,2048]{1,0:T(8,128)(2,1)}, bf16[512,2048]{1,0:T(8,128)(2,1)}, u32[]{:S(2)}, u32[]{:S(2)}) %collective-permute-start.5) | collective-permute-done | bytes 2097184 | tf_op jit(solution)/shard_map/ppermute | solution.py:21
  338.9 0.0 copy-done
  338.9 47.2 %query_side.1 = (bf16[512,2048]{1,0:T(8,128)(2,1)S(1)}, bf16[512,2048]{1,0:T(8,128)(2,1)}, f32[8,4,512]{2,1,0:T(4,128)S(1)}) custom-call(s32[4,5]{1,0:T(4,128)S(1)} %fusion.1.live_ref, bf16[512,2048]{1,0:T(8,128)(2,1)S(1)} %copy-done, bf16[512,2048]{1,0:T(8,128)(2,1)} %convolution_convert_fusion.2.g_ref.refs_1_, bf16[512,2048]{1,0:T(8,128)(2,1)} %k_ref.1, ...), custom_call_target="tpu_custom_call" | custom-call | flops 25769803776 | bytes 25165824 | tf_op jit(solution)/shard_map/query_side/pallas_call | solution.py:171
  386.1 1.3 copy-done.3
  387.4 0.0 copy-done.5
  387.4 12.5 %convolution_convert_fusion = bf16[2048,4096]{1,0:T(8,128)(2,1)} fusion(bf16[512,2048]{1,0:T(8,128)(2,1)S(1)} %get-tuple-element.10, bf16[512,4096]{1,0:T(8,128)(2,1)S(1)} %copy-done.5), kind=kOutput, calls=%fused_computation | convolution fusion | flops 8598323200 | bytes 23068672 | tf_op jit(solution)/shard_map/dot_general | solution.py:183
  400.0 0.0 reduce-scatter.5.cloned.1.call-update
  400.0 0.0 reduce-scatter.3.cloned.1.call-start
  400.0 14.5 %convolution_convert_fusion.1 = bf16[512,4096]{1,0:T(8,128)(2,1)} fusion(bf16[512,2048]{1,0:T(8,128)(2,1)} %copy-done.3, bf16[2048,4096]{1,0:T(8,128)(2,1)} %all-gather.2.cloned.1.call-done), kind=kOutput, calls=%fused_computation.1 | convolution fusion | flops 8592031744 | bytes 23068672 | tf_op jit(solution)/shard_map/dot_general | solution.py:189
  414.5 0.0 reduce-scatter.3.cloned.1.call-update
  414.6 1.9 collective-permute-start.9
  416.5 1.9 collective-permute-start.12
  418.4 1.9 collective-permute-start.15
  420.4 0.0 copy-done.4
  420.4 1.9 collective-permute-start.8
  422.3 2.6 collective-permute-start.7
  424.9 81.4 %collective-permute-done.8 = s32[4,5]{1,0:T(4,128)S(1)} collective-permute-done((s32[4,5]{1,0:T(4,128)S(1)}, s32[4,5]{1,0:T(4,128)S(1)}, u32[]{:S(2)}, u32[]{:S(2)}) %collective-permute-start.8) | collective-permute-done | bytes 112 | tf_op jit(solution)/shard_map/ppermute | solution.py:21
  506.3 10.8 %collective-permute-start.6 = (s32[4,5]{1,0:T(4,128)S(1)}, s32[4,5]{1,0:T(4,128)S(1)}, u32[]{:S(2)}, u32[]{:S(2)}) collective-permute-start(s32[4,5]{1,0:T(4,128)S(1)} %copy-done.4), channel_id=1, source_target_pairs={{2,0},{4,2},{6,4},{8,6},{10,8},{12,10},{14,12},{16,14},{18,16},{20... | collective-permute-start | bytes 248 | tf_op jit(solution)/shard_map/ppermute | solution.py:21
  517.2 61.9 %collective-permute-done.7 = s32[4,5]{1,0:T(4,128)S(1)} collective-permute-done((s32[4,5]{1,0:T(4,128)S(1)}, s32[4,5]{1,0:T(4,128)S(1)}, u32[]{:S(2)}, u32[]{:S(2)}) %collective-permute-start.7) | collective-permute-done | bytes 112 | tf_op jit(solution)/shard_map/ppermute | solution.py:21
  579.1 23.7 %collective-permute-start.10 = (bf16[512,2048]{1,0:T(8,128)(2,1)}, bf16[512,2048]{1,0:T(8,128)(2,1)S(1)}, u32[]{:S(2)}, u32[]{:S(2)}) collective-permute-start(bf16[512,2048]{1,0:T(8,128)(2,1)} %convolution_convert_fusion.2.g_ref.refs_1_), channel_id=1, source_target_pairs={{2,0},{4,2},{6,4},{8,6},{10,8},{12,10},{14,12},{16,14},{18,16},{20... | collective-permute-start | bytes 6291464 | tf_op jit(solution)/shard_map/ppermute | solution.py:21
  602.8 2.4 collective-permute-done.6
  605.2 1.9 collective-permute-start.13
  607.1 0.0 collective-permute-done.9.refs_3_
  607.1 0.0 copy-start.6
  607.1 2.1 collective-permute-start.16
  609.2 0.0 collective-permute-done.12.refs_6_
  609.2 0.0 copy-start.7
  609.3 1.9 collective-permute-start.11
  611.2 0.0 collective-permute-done.15.refs_9_
  611.2 0.0 copy-start.8
  611.2 3.1 collective-permute-start.14
  614.3 141.2 %collective-permute-done.11.refs_5_ = f32[8,4,512]{2,1,0:T(4,128)S(1)} collective-permute-done((f32[8,4,512]{2,1,0:T(4,128)S(1)}, f32[8,4,512]{2,1,0:T(4,128)S(1)}, u32[]{:S(2)}, u32[]{:S(2)}) %collective-permute-start.11) | collective-permute-done | bytes 65568 | tf_op jit(solution)/shard_map/ppermute | solution.py:21
  755.5 2.1 collective-permute-start.17
  757.6 0.0 collective-permute-done.14.refs_8_
  757.6 2.9 collective-permute-done.17.refs_11_
  760.5 0.0 collective-permute-done.10.refs_4_
  760.5 0.0 collective-permute-done.13.refs_7_
  760.5 0.0 copy-start.10
  760.5 1.4 copy-done.10
  761.9 0.0 collective-permute-done.16.refs_10_
  761.9 0.0 copy-done.8
  761.9 0.6 copy-done.9
  762.6 1.6 copy-done.1
  764.2 1.6 copy-done.2
  765.7 29.8 %key_side.1 = (bf16[512,2048]{1,0:T(8,128)(2,1)}, bf16[512,2048]{1,0:T(8,128)(2,1)}) custom-call(s32[16,5]{1,0:T(8,128)S(1)} %pad_add_fusion.link_ref, bf16[512,2048]{1,0:T(8,128)(2,1)S(1)} %copy-done.1, bf16[512,2048]{1,0:T(8,128)(2,1)S(1)} %copy-done.2, bf16[512,2048]{1,0:T(8,128)(2,1)} %refs_0_.3, ...), custom_call_target="tpu_custom_call" | custom-call | flops 25769803776 | bytes 25165824 | tf_op jit(solution)/shard_map/key_side/pallas_call | solution.py:197
  795.6 0.0 reduce-scatter.5.cloned.1.call-done
  795.6 2.7 convert_element_type.19
  (12 shorter events, 0.0 us)
Async XLA Ops:
  7.2 230.1 %all-gather.2.cloned.1.call-start = ((), (), s32[]{:S(2)}) async-start(), calls=%async_computation.2 | async-start | bytes 17825792 | tf_op jit(solution)/shard_map/all_gather | solution.py:145
  7.9 787.7 %reduce-scatter.5.cloned.1.call-start = ((), (), s32[]{:S(2)}) async-start(), calls=%async_computation.4 | async-start | bytes 17825792 | tf_op jit(solution)/shard_map/reduce_scatter | solution.py:186
  7.9 80.6 %collective-permute-start = (bf16[512,2048]{1,0:T(8,128)(2,1)}, bf16[512,2048]{1,0:T(8,128)(2,1)}, u32[]{:S(2)}, u32[]{:S(2)}) collective-permute-start(bf16[512,2048]{1,0:T(8,128)(2,1)} %k_ref.1), channel_id=1, source_target_pairs={{0,2},{2,4},{4,6},{6,8},{8,10},{10,12},{12,14},{14,16},{16,18},{18... | collective-permute-start | bytes 6291464 | tf_op jit(solution)/shard_map/ppermute | solution.py:21
  11.7 240.2 %collective-permute-start.2 = (bf16[512,2048]{1,0:T(8,128)(2,1)}, bf16[512,2048]{1,0:T(8,128)(2,1)}, u32[]{:S(2)}, u32[]{:S(2)}) collective-permute-start(bf16[512,2048]{1,0:T(8,128)(2,1)} %k_ref.1), channel_id=1, source_target_pairs={{0,4},{2,6},{4,8},{6,10},{8,12},{10,14},{12,16},{14,18},{16,20},{1... | collective-permute-start | bytes 6291464 | tf_op jit(solution)/shard_map/ppermute | solution.py:21
  14.8 237.0 %collective-permute-start.1 = (bf16[512,2048]{1,0:T(8,128)(2,1)}, bf16[512,2048]{1,0:T(8,128)(2,1)}, u32[]{:S(2)}, u32[]{:S(2)}) collective-permute-start(bf16[512,2048]{1,0:T(8,128)(2,1)} %v_ref.1), channel_id=1, source_target_pairs={{0,2},{2,4},{4,6},{6,8},{8,10},{10,12},{12,14},{14,16},{16,18},{18... | collective-permute-start | bytes 6291464 | tf_op jit(solution)/shard_map/ppermute | solution.py:21
  17.0 273.8 %collective-permute-start.3 = (bf16[512,2048]{1,0:T(8,128)(2,1)}, bf16[512,2048]{1,0:T(8,128)(2,1)}, u32[]{:S(2)}, u32[]{:S(2)}) collective-permute-start(bf16[512,2048]{1,0:T(8,128)(2,1)} %v_ref.1), channel_id=1, source_target_pairs={{0,4},{2,6},{4,8},{6,10},{8,12},{10,14},{12,16},{14,18},{16,20},{1... | collective-permute-start | bytes 6291464 | tf_op jit(solution)/shard_map/ppermute | solution.py:21
  20.2 296.2 %collective-permute-start.4 = (bf16[512,2048]{1,0:T(8,128)(2,1)}, bf16[512,2048]{1,0:T(8,128)(2,1)}, u32[]{:S(2)}, u32[]{:S(2)}) collective-permute-start(bf16[512,2048]{1,0:T(8,128)(2,1)} %k_ref.1), channel_id=1, source_target_pairs={{0,8},{2,10},{4,12},{6,14},{8,16},{10,18},{12,20},{14,22},{16,24},... | collective-permute-start | bytes 6291464 | tf_op jit(solution)/shard_map/ppermute | solution.py:21
  23.0 316.0 %copy-start = (bf16[512,2048]{1,0:T(8,128)(2,1)S(1)}, bf16[512,2048]{1,0:T(8,128)(2,1)}, u32[]{:S(2)}) copy-start(bf16[512,2048]{1,0:T(8,128)(2,1)} %refs_0_.3) | copy-start | bytes 6291460
  88.6 250.4 %collective-permute-start.5 = (bf16[512,2048]{1,0:T(8,128)(2,1)}, bf16[512,2048]{1,0:T(8,128)(2,1)}, u32[]{:S(2)}, u32[]{:S(2)}) collective-permute-start(bf16[512,2048]{1,0:T(8,128)(2,1)} %v_ref.1), channel_id=1, source_target_pairs={{0,8},{2,10},{4,12},{6,14},{8,16},{10,18},{12,20},{14,22},{16,24},... | collective-permute-start | bytes 6291464 | tf_op jit(solution)/shard_map/ppermute | solution.py:21
  251.9 135.6 %copy-start.5 = (bf16[512,4096]{1,0:T(8,128)(2,1)S(1)}, bf16[512,4096]{1,0:T(8,128)(2,1)}, u32[]{:S(2)}) copy-start(bf16[512,4096]{1,0:T(8,128)(2,1)} %param.11) | copy-start | bytes 12582916
  386.1 1.3 copy-start.3
  400.0 398.3 %reduce-scatter.3.cloned.1.call-start = ((), (), s32[]{:S(2)}) async-start(), calls=%async_computation.3 | async-start | bytes 6291456 | tf_op jit(solution)/shard_map/reduce_scatter | solution.py:190
  414.5 5.8 copy-start.4
  414.6 192.6 %collective-permute-start.9 = (bf16[512,2048]{1,0:T(8,128)(2,1)S(1)}, bf16[512,2048]{1,0:T(8,128)(2,1)S(1)}, u32[]{:S(2)}, u32[]{:S(2)}) collective-permute-start(bf16[512,2048]{1,0:T(8,128)(2,1)S(1)} %copy-done), channel_id=1, source_target_pairs={{2,0},{4,2},{6,4},{8,6},{10,8},{12,10},{14,12},{16,14},{18,16},{20... | collective-permute-start | bytes 6291464 | tf_op jit(solution)/shard_map/ppermute | solution.py:21
  416.5 192.7 %collective-permute-start.12 = (bf16[512,2048]{1,0:T(8,128)(2,1)S(1)}, bf16[512,2048]{1,0:T(8,128)(2,1)S(1)}, u32[]{:S(2)}, u32[]{:S(2)}) collective-permute-start(bf16[512,2048]{1,0:T(8,128)(2,1)S(1)} %copy-done), channel_id=1, source_target_pairs={{4,0},{6,2},{8,4},{10,6},{12,8},{14,10},{16,12},{18,14},{20,16},{2... | collective-permute-start | bytes 6291464 | tf_op jit(solution)/shard_map/ppermute | solution.py:21
  418.4 192.8 %collective-permute-start.15 = (bf16[512,2048]{1,0:T(8,128)(2,1)S(1)}, bf16[512,2048]{1,0:T(8,128)(2,1)S(1)}, u32[]{:S(2)}, u32[]{:S(2)}) collective-permute-start(bf16[512,2048]{1,0:T(8,128)(2,1)S(1)} %copy-done), channel_id=1, source_target_pairs={{8,0},{10,2},{12,4},{14,6},{16,8},{18,10},{20,12},{22,14},{24,16},... | collective-permute-start | bytes 6291464 | tf_op jit(solution)/shard_map/ppermute | solution.py:21
  420.4 86.0 %collective-permute-start.8 = (s32[4,5]{1,0:T(4,128)S(1)}, s32[4,5]{1,0:T(4,128)S(1)}, u32[]{:S(2)}, u32[]{:S(2)}) collective-permute-start(s32[4,5]{1,0:T(4,128)S(1)} %copy-done.4), channel_id=1, source_target_pairs={{8,0},{10,2},{12,4},{14,6},{16,8},{18,10},{20,12},{22,14},{24,16},... | collective-permute-start | bytes 248 | tf_op jit(solution)/shard_map/ppermute | solution.py:21
  422.3 156.8 %collective-permute-start.7 = (s32[4,5]{1,0:T(4,128)S(1)}, s32[4,5]{1,0:T(4,128)S(1)}, u32[]{:S(2)}, u32[]{:S(2)}) collective-permute-start(s32[4,5]{1,0:T(4,128)S(1)} %copy-done.4), channel_id=1, source_target_pairs={{4,0},{6,2},{8,4},{10,6},{12,8},{14,10},{16,12},{18,14},{20,16},{2... | collective-permute-start | bytes 248 | tf_op jit(solution)/shard_map/ppermute | solution.py:21
  506.3 98.9 %collective-permute-start.6 = (s32[4,5]{1,0:T(4,128)S(1)}, s32[4,5]{1,0:T(4,128)S(1)}, u32[]{:S(2)}, u32[]{:S(2)}) collective-permute-start(s32[4,5]{1,0:T(4,128)S(1)} %copy-done.4), channel_id=1, source_target_pairs={{2,0},{4,2},{6,4},{8,6},{10,8},{12,10},{14,12},{16,14},{18,16},{20... | collective-permute-start | bytes 248 | tf_op jit(solution)/shard_map/ppermute | solution.py:21
  579.1 181.4 %collective-permute-start.10 = (bf16[512,2048]{1,0:T(8,128)(2,1)}, bf16[512,2048]{1,0:T(8,128)(2,1)S(1)}, u32[]{:S(2)}, u32[]{:S(2)}) collective-permute-start(bf16[512,2048]{1,0:T(8,128)(2,1)} %convolution_convert_fusion.2.g_ref.refs_1_), channel_id=1, source_target_pairs={{2,0},{4,2},{6,4},{8,6},{10,8},{12,10},{14,12},{16,14},{18,16},{20... | collective-permute-start | bytes 6291464 | tf_op jit(solution)/shard_map/ppermute | solution.py:21
  605.2 155.3 %collective-permute-start.13 = (bf16[512,2048]{1,0:T(8,128)(2,1)}, bf16[512,2048]{1,0:T(8,128)(2,1)S(1)}, u32[]{:S(2)}, u32[]{:S(2)}) collective-permute-start(bf16[512,2048]{1,0:T(8,128)(2,1)} %convolution_convert_fusion.2.g_ref.refs_1_), channel_id=1, source_target_pairs={{4,0},{6,2},{8,4},{10,6},{12,8},{14,10},{16,12},{18,14},{20,16},{2... | collective-permute-start | bytes 6291464 | tf_op jit(solution)/shard_map/ppermute | solution.py:21
  607.1 154.8 %copy-start.6 = (bf16[512,2048]{1,0:T(8,128)(2,1)}, bf16[512,2048]{1,0:T(8,128)(2,1)S(1)}, u32[]{:S(2)}) copy-start(bf16[512,2048]{1,0:T(8,128)(2,1)S(1)} %collective-permute-done.9.refs_3_) | copy-start | bytes 6291460
  607.1 154.8 %collective-permute-start.16 = (bf16[512,2048]{1,0:T(8,128)(2,1)}, bf16[512,2048]{1,0:T(8,128)(2,1)}, u32[]{:S(2)}, u32[]{:S(2)}) collective-permute-start(bf16[512,2048]{1,0:T(8,128)(2,1)} %convolution_convert_fusion.2.g_ref.refs_1_), channel_id=1, source_target_pairs={{8,0},{10,2},{12,4},{14,6},{16,8},{18,10},{20,12},{22,14},{24,16},... | collective-permute-start | bytes 6291464 | tf_op jit(solution)/shard_map/ppermute | solution.py:21
  609.2 152.7 %copy-start.7 = (bf16[512,2048]{1,0:T(8,128)(2,1)}, bf16[512,2048]{1,0:T(8,128)(2,1)S(1)}, u32[]{:S(2)}) copy-start(bf16[512,2048]{1,0:T(8,128)(2,1)S(1)} %collective-permute-done.12.refs_6_) | copy-start | bytes 6291460
  609.3 146.2 %collective-permute-start.11 = (f32[8,4,512]{2,1,0:T(4,128)S(1)}, f32[8,4,512]{2,1,0:T(4,128)S(1)}, u32[]{:S(2)}, u32[]{:S(2)}) collective-permute-start(f32[8,4,512]{2,1,0:T(4,128)S(1)} %get-tuple-element.12.refs_2_), channel_id=1, source_target_pairs={{2,0},{4,2},{6,4},{8,6},{10,8},{12,10},{14,12},{16,14},{18,16},{20... | collective-permute-start | bytes 196616 | tf_op jit(solution)/shard_map/ppermute | solution.py:21
  611.2 150.7 %copy-start.8 = (bf16[512,2048]{1,0:T(8,128)(2,1)}, bf16[512,2048]{1,0:T(8,128)(2,1)S(1)}, u32[]{:S(2)}) copy-start(bf16[512,2048]{1,0:T(8,128)(2,1)S(1)} %collective-permute-done.15.refs_9_) | copy-start | bytes 6291460
  611.2 146.4 %collective-permute-start.14 = (f32[8,4,512]{2,1,0:T(4,128)S(1)}, f32[8,4,512]{2,1,0:T(4,128)S(1)}, u32[]{:S(2)}, u32[]{:S(2)}) collective-permute-start(f32[8,4,512]{2,1,0:T(4,128)S(1)} %get-tuple-element.12.refs_2_), channel_id=1, source_target_pairs={{4,0},{6,2},{8,4},{10,6},{12,8},{14,10},{16,12},{18,14},{20,16},{2... | collective-permute-start | bytes 196616 | tf_op jit(solution)/shard_map/ppermute | solution.py:21
  755.5 5.0 collective-permute-start.17
  760.5 2.1 copy-start.9
  760.5 1.4 copy-start.10
  762.6 1.6 copy-start.1
  764.2 1.6 copy-start.2
Sparse Core Ops, SparseCore 0:
  10.2 227.0 all-gather.1
  400.1 275.6 reduce-scatter.4
  678.7 55.7 reduce-scatter.2

commit v2 on v0

v2 whole, which is shorter than its diff:
```python
import functools
import math

import jax
import jax.numpy as jnp
from jax import lax
from jax.experimental import pallas as pl
from jax.experimental.pallas import tpu as pltpu
from jax.sharding import PartitionSpec as P

HEAD_DIM = 128
BLK = 128
LEVELS = 5
PIECES = 4
DEAD = -1e30


def passed_along(block, axis, distance):
    devices = range(lax.axis_size(axis))
    route = [(i - distance, i) for i in devices if i - distance in devices]
    return lax.ppermute(block, axis, route)


def rows_of(block):
    return slice(block * BLK, (block + 1) * BLK)


def dot_nt(a, b):
    return lax.dot_general(a, b, (((1,), (1,)), ((), ())), preferred_element_type=jnp.float32)


def dot_nn(a, b):
    return lax.dot_general(a, b, (((1,), (0,)), ((), ())), preferred_element_type=jnp.float32)


def dot_tn(a, b):
    return lax.dot_general(a, b, (((0,), (0,)), ((), ())), preferred_element_type=jnp.float32)


def one_head(scale, at_ref, live_ref, q_ref, g_ref, kv_ref, old_ref, att_ref, dq_ref, dkv_ref, dold_ref, dk_acc, dv_acc):
    at = at_ref[0]
    pieces, length, _ = q_ref.shape
    count = length // BLK
    blocks = pieces * count
    causal = lax.broadcasted_iota(jnp.int32, (BLK, BLK), 0) >= lax.broadcasted_iota(
        jnp.int32, (BLK, BLK), 1
    )

    def load(member, block):
        ref = kv_ref if block >= 0 else old_ref
        block = block % blocks
        return ref[member, (block // count) ^ at, rows_of(block % count), :]

    dk_acc[...] = jnp.zeros_like(dk_acc)
    dv_acc[...] = jnp.zeros_like(dv_acc)
    for t in range(blocks):
        here, rows = (t // count) ^ at, rows_of(t % count)
        q = q_ref[here, rows, :]
        g = g_ref[here, rows, :]
        where = [t] + [t - 2**l for l in range(LEVELS)]
        kc = jnp.concatenate([load(0, c) for c in where], 0)
        vc = jnp.concatenate([load(1, c) for c in where], 0)
        s = dot_nt(q, kc) * scale
        parts = [jnp.where(causal, s[:, :BLK], DEAD)]
        for l in range(LEVELS):
            part = s[:, (l + 1) * BLK : (l + 2) * BLK]
            parts.append(jnp.where(live_ref[t, l] > 0, part, DEAD))
        s = jnp.concatenate(parts, 1)
        top = jnp.max(s, axis=1, keepdims=True)
        w = jnp.exp(s - top)
        prob = w * (1.0 / jnp.sum(w, axis=1, keepdims=True))
        low = prob.astype(jnp.bfloat16)
        att = dot_nn(low, vc).astype(jnp.bfloat16)
        att_ref[here, rows, :] = att
        delta = jnp.sum(g.astype(jnp.float32) * att.astype(jnp.float32), axis=1, keepdims=True)
        ds = (prob * ((dot_nt(g, vc) - delta) * scale)).astype(jnp.bfloat16)
        dq_ref[here, rows, :] = dot_nn(ds, kc).astype(jnp.bfloat16)
        dk = dot_tn(ds, q)
        dv = dot_tn(low, g)
        for n, c in enumerate(where):
            dk_acc[rows_of(c + blocks), :] += dk[rows_of(n), :]
            dv_acc[rows_of(c + blocks), :] += dv[rows_of(n), :]
    for member, acc in enumerate((dk_acc, dv_acc)):
        for p in range(pieces):
            old = slice(p * length, (p + 1) * length)
            own = slice((pieces + p) * length, (pieces + p + 1) * length)
            dold_ref[member, p ^ at, :, :] = acc[old, :].astype(jnp.bfloat16)
            dkv_ref[member, p ^ at, :, :] = acc[own, :].astype(jnp.bfloat16)


def exchanged(block, bit):
    return lax.ppermute(block, "ctx", [(i, i ^ bit) for i in range(lax.axis_size("ctx"))])


def by_distance(grad_mixed):
    rows, width = grad_mixed.shape
    count = lax.axis_size("ctx")
    planes = count // 4
    chunk = width // count
    me = lax.axis_index("ctx")
    plane, side, core = me // 4, (me // 2) % 2, me % 2

    def picked(which):
        owners = [
            ((plane + step) % planes) * 4 + other * 2 + which
            for other in (1 - side, side)
            for step in range(1, planes + 1)
        ]
        return jnp.concatenate(
            [lax.dynamic_slice_in_dim(grad_mixed, owner * chunk, chunk, 1) for owner in owners], 1
        )

    return picked(1 - core), picked(core)


def weight_gradient(attended, columns):
    count = lax.axis_size("ctx")
    planes = count // 4
    chunk = columns[0].shape[1] // (2 * planes)

    def product(picked):
        return lax.dot_general(
            attended, picked, (((0,), (0,)), ((), ())), preferred_element_type=jnp.float32
        ).astype(jnp.bfloat16)

    half = planes * chunk
    arrived = exchanged(product(columns[0]), 1)
    mine = product(columns[1])
    away = (
        mine[:, :half].astype(jnp.float32) + arrived[:, :half].astype(jnp.float32)
    ).astype(jnp.bfloat16)
    came = exchanged(away, 2)
    kept = (
        mine[:, half:].astype(jnp.float32)
        + arrived[:, half:].astype(jnp.float32)
        + came.astype(jnp.float32)
    )
    total = kept[:, (planes - 1) * chunk :]
    sent = kept[:, : (planes - 1) * chunk].astype(jnp.bfloat16)
    for step in range(1, planes):
        part = lax.ppermute(
            sent[:, (step - 1) * chunk : step * chunk],
            "ctx",
            [(i, (i + 4 * step) % count) for i in range(count)],
        )
        total = total + part.astype(jnp.float32)
    return total


def summed_over_heads(attended, weight_full):
    count = lax.axis_size("head")
    me = lax.axis_index("head")
    width = weight_full.shape[1] // count

    def product(which):
        columns = lax.dynamic_slice_in_dim(weight_full, which * width, width, 1)
        return jnp.dot(attended, columns, preferred_element_type=jnp.float32).astype(jnp.bfloat16)

    parts = []
    for step in range(1, count):
        away = product((me + step) % count)
        parts.append(
            lax.ppermute(away, "head", [(i, (i + step) % count) for i in range(count)])
        )
    total = product(me).astype(jnp.float32)
    for part in parts:
        total = total + part.astype(jnp.float32)
    return total.astype(jnp.bfloat16)


def placed_piece(at_ref, from_ref, to_ref):
    to_ref[...] = from_ref[0]


def on_device(queries, key_rows, values, out_weight, grad_mixed, link_mask):
    row_count, col_count = queries.shape
    blk_count = row_count // BLK
    wide = col_count // PIECES
    score_scale = 1.0 / math.sqrt(HEAD_DIM)
    me = lax.axis_index("ctx")
    at = me % PIECES
    others = at ^ jnp.arange(PIECES, dtype=jnp.int32)

    def columns_for(array, piece):
        return lax.dynamic_slice_in_dim(array, (at ^ piece) * wide, wide, 1)

    def to_heads(arrays):
        got = []
        for piece in range(PIECES):
            part = jnp.stack([columns_for(array, piece) for array in arrays], 0)
            got.append(exchanged(part, piece) if piece else part)
        return jnp.stack(got, 1)

    def to_steps(array):
        got = [exchanged(array[piece], piece) if piece else array[piece] for piece in range(PIECES)]
        return pl.pallas_call(
            placed_piece,
            grid_spec=pltpu.PrefetchScalarGridSpec(
                num_scalar_prefetch=1,
                grid=(PIECES,),
                in_specs=[
                    pl.BlockSpec((1, row_count, wide), lambda i, at_ref: (i ^ at_ref[0], 0, 0))
                ],
                out_specs=pl.BlockSpec((row_count, wide), lambda i, at_ref: (0, i)),
            ),
            out_shape=jax.ShapeDtypeStruct((row_count, col_count), jnp.bfloat16),
            name="placed_piece",
        )(at.astype(jnp.int32).reshape(1), jnp.stack(got, 0))

    kv = to_heads([key_rows, values])
    old = passed_along(kv, "ctx", PIECES)
    (query_pieces,) = to_heads([queries])
    links = jnp.stack([exchanged(link_mask, p) if p else link_mask for p in range(PIECES)], 0)
    links = jnp.take(links, others, axis=0).reshape(PIECES * blk_count, LEVELS)
    first = (me // PIECES) * PIECES * blk_count
    block_ids = first + jnp.arange(PIECES * blk_count, dtype=jnp.int32)
    span_array = jnp.array([2**l for l in range(LEVELS)], jnp.int32)
    live = ((block_ids[:, None] - span_array[None, :] >= 0) & (links == 1)).astype(jnp.int32)

    weight_full = lax.all_gather(out_weight, "ctx", axis=1, tiled=True)
    columns = by_distance(grad_mixed)
    weight_full, old, query_pieces, columns, live = lax.optimization_barrier(
        (weight_full, old, query_pieces, columns, live)
    )
    grad_attn = lax.dot_general(
        grad_mixed, weight_full, (((1,), (1,)), ((), ())), preferred_element_type=jnp.float32
    ).astype(jnp.bfloat16)
    (grad_pieces,) = to_heads([grad_attn])

    single = pl.BlockSpec((PIECES, row_count, HEAD_DIM), lambda i: (0, 0, i))
    double = pl.BlockSpec((2, PIECES, row_count, HEAD_DIM), lambda i: (0, 0, 0, i))
    scalars = pl.BlockSpec(memory_space=pltpu.SMEM)
    like_single = jax.ShapeDtypeStruct(query_pieces.shape, jnp.bfloat16)
    like_double = jax.ShapeDtypeStruct(kv.shape, jnp.bfloat16)
    heads = wide // HEAD_DIM
    tiles = PIECES * blk_count * heads * (LEVELS + 1)
    attended, grad_query, grad_kv, grad_old = pl.pallas_call(
        functools.partial(one_head, score_scale),
        grid=(heads,),
        in_specs=[scalars, scalars, single, single, double, double],
        out_specs=[single, single, double, double],
        out_shape=[like_single, like_single, like_double, like_double],
        scratch_shapes=[pltpu.VMEM((2 * PIECES * row_count, HEAD_DIM), jnp.float32)] * 2,
        compiler_params=pltpu.CompilerParams(vmem_limit_bytes=48 * 1024 * 1024),
        cost_estimate=pl.CostEstimate(
            flops=6 * 2 * tiles * BLK * BLK * HEAD_DIM * 4,
            bytes_accessed=12 * row_count * col_count * 2,
            transcendentals=tiles * BLK * BLK,
        ),
        name="one_head",
    )(at.astype(jnp.int32).reshape(1), live, query_pieces, grad_pieces, kv, old)

    attended, grad_query, grad_kv, grad_old = lax.optimization_barrier(
        (to_steps(attended), grad_query, grad_kv, grad_old)
    )
    owed = passed_along(grad_old, "ctx", -PIECES)
    grad_out_weight = weight_gradient(attended, columns)
    mixed_out = summed_over_heads(attended, weight_full)
    grad_query = to_steps(grad_query)
    total = (grad_kv.astype(jnp.float32) + owed.astype(jnp.float32)).astype(jnp.bfloat16)
    return (mixed_out, grad_query, to_steps(total[0]), to_steps(total[1]), grad_out_weight)


def solution(mesh):
    placed = (
        P("ctx", "head"),
        P("ctx", "head"),
        P("ctx", "head"),
        P("head", "ctx"),
        P("ctx", None),
        P("ctx", None),
    )
    return jax.shard_map(
        on_device,
        mesh=mesh,
        in_specs=placed,
        out_specs=(
            P("ctx", "head"),
            P("ctx", "head"),
            P("ctx", "head"),
            P("ctx", "head"),
            P("head", "ctx"),
        ),
        check_vma=False,
    )
```

time: 833 us -> 626 us (0.75)
  local copies, waits for them, and re-layouts: 123 us -> 18.5 us
  matrix products: 147 us -> 48.1 us
  waiting for transfers between devices: 471 us -> 393 us
  Pallas kernels: 0 us -> 71.6 us
    ppermute x12 -> x2, waiting for transfers between devices: 470 us -> 154 us  [passed_along(): return lax.ppermute(block, axis, route)]
    ppermute x0 -> x30, waiting for transfers between devices: none -> 239 us  [the longest x26 193 us: exchanged(): lax.ppermute(block, 'ctx', [(i, i ^ bit) for i in range(lax.axis_size('ct...]
    dot_general x8 -> x4, matrix products: 133 us -> 34.5 us  [the longest x2 19.3 us: product(): jnp.dot(attended, columns, preferred_element_type=jnp.float32)]
    pallas_call x0 -> x5, Pallas kernels: none -> 71.6 us  [the longest x1 56.3 us: on_device(): pl.pallas_call(functools.partial(one_head, score_scale), grid=(heads,), i...]
    unnamed x72 -> x49, local copies, waits for them, and re-layouts: 44.4 us -> 9.12 us
    convert_element_type x6 -> x0, local copies, waits for them, and re-layouts: 24.9 us -> none  [the longest x2 12.8 us: short(): return part.astype(jnp.bfloat16) if part.dtype == jnp.float32 else part]
    ppermute x12 -> x2, starting transfers between devices: 30 us -> 5.23 us  [passed_along(): return lax.ppermute(block, axis, route)]
    ppermute x0 -> x30, starting transfers between devices: none -> 23.8 us  [the longest x26 20.2 us: exchanged(): lax.ppermute(block, 'ctx', [(i, i ^ bit) for i in range(lax.axis_size('ct...]
  transfers between devices with their start and end apart: 15 -> 33, of which waited for: 11 -> 20; matrix products, arithmetic and copies ran while one was open for 31% -> 12% of each run, Pallas kernels for 0% -> 2%
where the time goes in v2:
time: 626 us; the launch traced here: 615 us
  waiting for transfers between devices  393 us (63%)
  Pallas kernels  71.6 us (11%)
  matrix products  48.1 us (8%)
  other arithmetic  39.7 us (6%)
  starting transfers between devices  29.1 us (5%)
  local copies, waits for them, and re-layouts  18.5 us (3%)
  between operations  14.8 us (2%)
    ppermute x26, waiting for transfers between devices, exchanged(): lax.ppermute(block, 'ctx', [(i, i ^ bit) for i in range(lax.axis_size('ct...  193 us
    ppermute x2, waiting for transfers between devices, passed_along(): return lax.ppermute(block, axis, route)  154 us
    pallas_call x1, Pallas kernels, on_device(): pl.pallas_call(functools.partial(one_head, score_scale), grid=(heads,), i...  56.3 us
    ppermute x3, waiting for transfers between devices, weight_gradient(): lax.ppermute(sent[:, (step - 1) * chunk:step * chunk], 'ctx', [(i, (i + 4...  45.8 us
    ppermute x26, starting transfers between devices, exchanged(): lax.ppermute(block, 'ctx', [(i, i ^ bit) for i in range(lax.axis_size('ct...  20.2 us
    dot_general x2, matrix products, product(): jnp.dot(attended, columns, preferred_element_type=jnp.float32)  19.3 us
    pallas_call x4, Pallas kernels, to_steps(): pl.pallas_call(placed_piece, grid_spec=pltpu.PrefetchScalarGridSpec(num_s...  15.3 us
    dot_general x2, matrix products, product(): lax.dot_general(attended, picked, (((0,), (0,)), ((), ())), preferred_ele...  15.2 us
  transfers between devices with their start and end apart: 33, of which 20 were waited for; matrix products, arithmetic and copies ran while one was open for 12% of the time, Pallas kernels for 2%

profile of v2, /device:TPU:15, one launch (start us, length us, event | category | flops | bytes accessed | tf_op | source)
XLA Modules:
  0.0 614.9 jit_solution(13359142128056352657)
XLA Ops:
  7.9 2.5 dynamic-slice_bitcast_fusion.14
  11.5 1.3 collective-permute-start.1
  13.1 34.4 %collective-permute-done.2 = bf16[2,512,512]{2,1,0:T(8,128)(2,1)S(1)} collective-permute-done((bf16[2,512,512]{2,1,0:T(8,128)(2,1)S(1)}, bf16[2,512,512]{2,1,0:T(8,128)(2,1)S(1)}, u32[]{:S(2)}, u32[]{:S(2)}) %collective-permute-start.2) | collective-permute-done | bytes 1048608 | tf_op jit(solution)/shard_map/ppermute | solution.py:92
  47.5 22.5 %collective-permute-done.1 = bf16[2,512,512]{2,1,0:T(8,128)(2,1)S(1)} collective-permute-done((bf16[2,512,512]{2,1,0:T(8,128)(2,1)S(1)}, bf16[2,512,512]{2,1,0:T(8,128)(2,1)S(1)}, u32[]{:S(2)}, u32[]{:S(2)}) %collective-permute-start.1) | collective-permute-done | bytes 1048608 | tf_op jit(solution)/shard_map/ppermute | solution.py:92
  70.0 2.3 pad_maximum_fusion.kv_ref
  72.3 3.3 collective-permute-start.3
  77.5 1.2 collective-permute-start.5
  79.4 1.3 dynamic-slice_dynamic-update-slice_fusion.7
  80.7 1.4 dynamic-slice_dynamic-update-slice_fusion.6
  82.1 1.1 dynamic-slice_dynamic-update-slice_fusion.5
  83.2 1.1 dynamic-slice_dynamic-update-slice_fusion.4
  84.7 1.3 copy-done.12
  86.0 1.3 copy-done.14
  87.4 37.9 %collective-permute-done.9 = s32[4,5]{1,0:T(4,128)S(1)} collective-permute-done((s32[4,5]{1,0:T(4,128)S(1)}, s32[4,5]{1,0:T(4,128)S(1)}, u32[]{:S(2)}, u32[]{:S(2)}) %collective-permute-start.9) | collective-permute-done | bytes 112 | tf_op jit(solution)/shard_map/ppermute | solution.py:92
  125.6 2.5 collective-permute-done.8
  128.1 1.0 collective-permute-start.7
  130.6 1.6 maximum_bitcast_fusion.q_ref
  132.2 101.1 %collective-permute-done.3.old_ref = bf16[2,4,512,512]{3,2,1,0:T(8,128)(2,1)} collective-permute-done((bf16[2,4,512,512]{3,2,1,0:T(8,128)(2,1)}, bf16[2,4,512,512]{3,2,1,0:T(8,128)(2,1)}, u32[]{:S(2)}, u32[]{:S(2)}) %collective-permute-start.3) | collective-permute-done | bytes 4194336 | tf_op jit(solution)/shard_map/ppermute | solution.py:21
  233.3 13.6 %convolution_convert_fusion.2 = bf16[2048,512]{0,1:T(8,128)(2,1)S(1)} fusion(bf16[2048,4096]{1,0:T(8,128)(2,1)} %all-gather.2.cloned.1.call-done, bf16[512,4096]{1,0:T(8,128)(2,1)} %param.11), kind=kOutput, calls=%fused_computation.14 | convolution fusion | flops 8590983168 | bytes 23068672 | tf_op jit(solution)/shard_map/dot_general | solution.py:225
  248.2 1.2 collective-permute-start.11
  249.4 12.3 %collective-permute-done.12 = bf16[1,512,512]{2,1,0:T(8,128)(2,1)S(1)} collective-permute-done((bf16[1,512,512]{2,1,0:T(8,128)(2,1)S(1)}, bf16[1,512,512]{2,1,0:T(8,128)(2,1)S(1)}, u32[]{:S(2)}, u32[]{:S(2)}) %collective-permute-start.12) | collective-permute-done | bytes 524320 | tf_op jit(solution)/shard_map/ppermute | solution.py:92
  261.7 11.2 %collective-permute-done.11 = bf16[1,512,512]{2,1,0:T(8,128)(2,1)S(1)} collective-permute-done((bf16[1,512,512]{2,1,0:T(8,128)(2,1)S(1)}, bf16[1,512,512]{2,1,0:T(8,128)(2,1)S(1)}, u32[]{:S(2)}, u32[]{:S(2)}) %collective-permute-start.11) | collective-permute-done | bytes 524320 | tf_op jit(solution)/shard_map/ppermute | solution.py:92
  273.0 1.6 maximum_bitcast_fusion.1.g_ref
  274.6 56.3 %one_head.1 = (bf16[4,512,512]{2,1,0:T(8,128)(2,1)S(1)}, bf16[4,512,512]{2,1,0:T(8,128)(2,1)S(1)}, bf16[2,4,512,512]{3,2,1,0:T(8,128)(2,1)}, bf16[2,4,512,512]{3,2,1,0:T(8,128)(2,1)}) custom-call(s32[1]{0:T(128)} %bitcast.at_ref, s32[16,5]{1,0:T(8,128)S(1)} %fusion.15.live_ref, bf16[4,512,512]{2,1,0:T(8,128)(2,1)} %maximum_bitcast_fusion.q_ref, ...), custom_call_target="tpu_custom_call" | custom-call | flops 38654705664 | bytes 25165824 | tf_op jit(solution)/shard_map/one_head/pallas_call | solution.py:237
  331.8 1.1 collective-permute-start.14
  333.2 12.1 %collective-permute-done.15 = bf16[512,512]{1,0:T(8,128)(2,1)S(1)} collective-permute-done((bf16[512,512]{1,0:T(8,128)(2,1)S(1)}, bf16[512,512]{1,0:T(8,128)(2,1)S(1)}, u32[]{:S(2)}, u32[]{:S(2)}) %collective-permute-start.15) | collective-permute-done | bytes 524320 | tf_op jit(solution)/shard_map/ppermute | solution.py:92
  345.3 11.0 %collective-permute-done.14 = bf16[512,512]{1,0:T(8,128)(2,1)S(1)} collective-permute-done((bf16[512,512]{1,0:T(8,128)(2,1)S(1)}, bf16[512,512]{1,0:T(8,128)(2,1)S(1)}, u32[]{:S(2)}, u32[]{:S(2)}) %collective-permute-start.14) | collective-permute-done | bytes 524320 | tf_op jit(solution)/shard_map/ppermute | solution.py:92
  356.3 1.6 pad_maximum_fusion.1.from_ref
  357.9 3.8 placed_piece.4
  361.6 10.2 %convolution_convert_fusion = bf16[2048,2048]{1,0:T(8,128)(2,1)} fusion(bf16[512,2048]{1,0:T(8,128)(2,1)} %placed_piece.4, bf16[512,2048]{1,0:T(8,128)(2,1)} %copy-done.14), kind=kOutput, calls=%fused_computation.8 | convolution fusion | flops 4299161600 | bytes 12582912 | tf_op jit(solution)/shard_map/dot_general | solution.py:122
  372.5 1.9 collective-permute-start.20
  374.5 5.0 convolution_convert_fusion.1
  379.5 6.0 collective-permute-done.27
  385.5 4.0 add_convert_fusion
  389.5 1.3 copy-done
  391.2 9.8 %fusion.7 = bf16[512,2048]{1,0:T(8,128)(2,1)} fusion(bf16[512,2048]{1,0:T(8,128)(2,1)} %placed_piece.4, bf16[2048,4096]{1,0:T(8,128)(2,1)} %all-gather.2.cloned.1.call-done, s32[]{:T(128)S(6)} %select_n.200), kind=kOutput, calls=%fused_computation.13 | convolution fusion | flops 4296015872 | bytes 12582916 | tf_op jit(solution)/shard_map/dot_general | solution.py:157
  401.1 1.4 fusion.19
  402.5 2.1 collective-permute-start.19
  404.7 9.5 %fusion.4 = bf16[512,2048]{1,0:T(8,128)(2,1)} fusion(bf16[512,2048]{1,0:T(8,128)(2,1)S(1)} %copy-done.5, bf16[2048,4096]{1,0:T(8,128)(2,1)} %all-gather.2.cloned.1.call-done, s32[]{:T(128)S(6)} %select_n.198), kind=kOutput, calls=%fused_computation.12 | convolution fusion | flops 4296015872 | bytes 12582916 | tf_op jit(solution)/shard_map/dot_general | solution.py:157
  414.2 52.7 %collective-permute-done.20 = bf16[2,4,512,512]{3,2,1,0:T(8,128)(2,1)} collective-permute-done((bf16[2,4,512,512]{3,2,1,0:T(8,128)(2,1)}, bf16[2,4,512,512]{3,2,1,0:T(8,128)(2,1)}, u32[]{:S(2)}, u32[]{:S(2)}) %collective-permute-start.20) | collective-permute-done | bytes 4194336 | tf_op jit(solution)/shard_map/ppermute | solution.py:21
  467.7 4.7 add_convert_fusion.1
  472.4 1.4 slice_bitcast_fusion.3
  473.9 9.1 %collective-permute-done.28 = bf16[2048,1024]{1,0:T(8,128)(2,1)} collective-permute-done((bf16[2048,1024]{1,0:T(8,128)(2,1)}, bf16[2048,1024]{1,0:T(8,128)(2,1)}, u32[]{:S(2)}, u32[]{:S(2)}) %collective-permute-start.28) | collective-permute-done | bytes 4194336 | tf_op jit(solution)/shard_map/ppermute | solution.py:92
  482.9 2.3 collective-permute-start.23
  485.2 7.0 %fusion.17 = (bf16[2048,1024]{1,0:T(8,128)(2,1)S(1)}, f32[2048,1024]{1,0:T(8,128)}) fusion(bf16[2048,1024]{1,0:T(8,128)(2,1)} %collective-permute-done.28, bf16[2048,2048]{1,0:T(8,128)(2,1)S(1)} %bitcast.112, bf16[2048,2048]{1,0:T(8,128)(2,1)S(1)} %bitcast.114), kind=kLoop, calls=%fused_computation.87 | loop fusion | flops 12582912 | bytes 25165824 | tf_op jit(solution)/shard_map/convert
  492.3 3.2 collective-permute-done.19
  495.9 9.5 %collective-permute-done.18 = bf16[512,512]{1,0:T(8,128)(2,1)} collective-permute-done((bf16[512,512]{1,0:T(8,128)(2,1)}, bf16[512,512]{1,0:T(8,128)(2,1)}, u32[]{:S(2)}, u32[]{:S(2)}) %collective-permute-start.18) | collective-permute-done | bytes 524320 | tf_op jit(solution)/shard_map/ppermute | solution.py:92
  505.4 2.0 collective-permute-start.21
  507.7 1.9 fusion.18
  509.6 8.7 %collective-permute-done.23 = bf16[512,512]{1,0:T(8,128)(2,1)S(1)} collective-permute-done((bf16[512,512]{1,0:T(8,128)(2,1)S(1)}, bf16[512,512]{1,0:T(8,128)(2,1)S(1)}, u32[]{:S(2)}, u32[]{:S(2)}) %collective-permute-start.23) | collective-permute-done | bytes 524320 | tf_op jit(solution)/shard_map/ppermute | solution.py:92
  518.2 2.2 collective-permute-start.30
  520.5 7.4 %collective-permute-done.22 = bf16[512,512]{1,0:T(8,128)(2,1)S(1)} collective-permute-done((bf16[512,512]{1,0:T(8,128)(2,1)S(1)}, bf16[512,512]{1,0:T(8,128)(2,1)S(1)}, u32[]{:S(2)}, u32[]{:S(2)}) %collective-permute-start.22) | collective-permute-done | bytes 524320 | tf_op jit(solution)/shard_map/ppermute | solution.py:92
  527.9 1.3 collective-permute-start.29
  529.2 2.9 pad_maximum_fusion.2.from_ref
  532.1 3.9 placed_piece.5
  536.3 4.4 collective-permute-done.26
  540.7 3.8 add_convert_fusion.2
  544.5 2.6 pad_maximum_fusion.3.from_ref
  547.1 3.8 placed_piece.6
  550.9 2.9 pad_maximum_fusion.4.from_ref
  553.8 3.8 placed_piece.7
  557.6 23.3 %collective-permute-done.30 = bf16[2048,256]{1,0:T(8,128)(2,1)} collective-permute-done((bf16[2048,256]{1,0:T(8,128)(2,1)}, bf16[2048,256]{1,0:T(8,128)(2,1)}, u32[]{:S(2)}, u32[]{:S(2)}) %collective-permute-start.30) | collective-permute-done | bytes 1048608 | tf_op jit(solution)/shard_map/ppermute | solution.py:141
  581.0 22.4 %collective-permute-done.29 = bf16[2048,256]{1,0:T(8,128)(2,1)} collective-permute-done((bf16[2048,256]{1,0:T(8,128)(2,1)}, bf16[2048,256]{1,0:T(8,128)(2,1)}, u32[]{:S(2)}, u32[]{:S(2)}) %collective-permute-start.29) | collective-permute-done | bytes 1048608 | tf_op jit(solution)/shard_map/ppermute | solution.py:141
  603.4 4.2 fusion.11
  (97 shorter events, 12.5 us)
Async XLA Ops:
  7.2 226.2 %all-gather.2.cloned.1.call-start = ((), (), s32[]{:S(2)}) async-start(), calls=%async_computation | async-start | bytes 17825792 | tf_op jit(solution)/shard_map/all_gather | solution.py:220
  10.5 37.0 %collective-permute-start.2 = (bf16[2,512,512]{2,1,0:T(8,128)(2,1)S(1)}, bf16[2,512,512]{2,1,0:T(8,128)(2,1)S(1)}, u32[]{:S(2)}, u32[]{:S(2)}) collective-permute-start(bf16[2,512,512]{2,1,0:T(8,128)(2,1)S(1)} %pad_maximum_fusion.7), channel_id=1, source_target_pairs={{0,6},{2,4},{4,2},{6,0},{8,14},{10,12},{12,10},{14,8},{16,22},{18,... | collective-permute-start | bytes 3145736 | tf_op jit(solution)/shard_map/ppermute | solution.py:92
  11.5 58.5 %collective-permute-start.1 = (bf16[2,512,512]{2,1,0:T(8,128)(2,1)S(1)}, bf16[2,512,512]{2,1,0:T(8,128)(2,1)S(1)}, u32[]{:S(2)}, u32[]{:S(2)}) collective-permute-start(bf16[2,512,512]{2,1,0:T(8,128)(2,1)S(1)} %pad_maximum_fusion.6), channel_id=1, source_target_pairs={{0,4},{2,6},{4,0},{6,2},{8,12},{10,14},{12,8},{14,10},{16,20},{18,... | collective-permute-start | bytes 3145736 | tf_op jit(solution)/shard_map/ppermute | solution.py:92
  12.9 57.1 %collective-permute-start = (bf16[2,512,512]{2,1,0:T(8,128)(2,1)S(1)}, bf16[2,512,512]{2,1,0:T(8,128)(2,1)S(1)}, u32[]{:S(2)}, u32[]{:S(2)}) collective-permute-start(bf16[2,512,512]{2,1,0:T(8,128)(2,1)S(1)} %pad_maximum_fusion.5), channel_id=1, source_target_pairs={{0,2},{2,0},{4,6},{6,4},{8,10},{10,8},{12,14},{14,12},{16,18},{18,... | collective-permute-start | bytes 3145736 | tf_op jit(solution)/shard_map/ppermute | solution.py:92
  70.0 5.6 copy-start.6
  72.3 6.5 %copy-start.15 = (s32[4,5]{1,0:T(4,128)S(1)}, s32[4,5]{1,0:T(4,128)}, u32[]{:S(2)}) copy-start(s32[4,5]{1,0:T(4,128)} %param.12) | copy-start | bytes 244
  72.3 161.1 %collective-permute-start.3 = (bf16[2,4,512,512]{3,2,1,0:T(8,128)(2,1)}, bf16[2,4,512,512]{3,2,1,0:T(8,128)(2,1)}, u32[]{:S(2)}, u32[]{:S(2)}) collective-permute-start(bf16[2,4,512,512]{3,2,1,0:T(8,128)(2,1)} %pad_maximum_fusion.kv_ref), channel_id=1, source_target_pairs={{0,8},{2,10},{4,12},{6,14},{8,16},{10,18},{12,20},{14,22},{16,24},... | collective-permute-start | bytes 12582920 | tf_op jit(solution)/shard_map/ppermute | solution.py:21
  76.7 54.0 %collective-permute-start.6 = (bf16[1,512,512]{2,1,0:T(8,128)(2,1)}, bf16[1,512,512]{2,1,0:T(8,128)(2,1)S(1)}, u32[]{:S(2)}, u32[]{:S(2)}) collective-permute-start(bf16[1,512,512]{2,1,0:T(8,128)(2,1)} %get-tuple-element.76), channel_id=1, source_target_pairs={{0,6},{2,4},{4,2},{6,0},{8,14},{10,12},{12,10},{14,8},{16,22},{18,... | collective-permute-start | bytes 1572872 | tf_op jit(solution)/shard_map/ppermute | solution.py:92
  77.5 53.1 %collective-permute-start.5 = (bf16[1,512,512]{2,1,0:T(8,128)(2,1)S(1)}, bf16[1,512,512]{2,1,0:T(8,128)(2,1)S(1)}, u32[]{:S(2)}, u32[]{:S(2)}) collective-permute-start(bf16[1,512,512]{2,1,0:T(8,128)(2,1)S(1)} %get-tuple-element.77), channel_id=1, source_target_pairs={{0,4},{2,6},{4,0},{6,2},{8,12},{10,14},{12,8},{14,10},{16,20},{18,... | collective-permute-start | bytes 1572872 | tf_op jit(solution)/shard_map/ppermute | solution.py:92
  78.7 51.9 %collective-permute-start.4 = (bf16[1,512,512]{2,1,0:T(8,128)(2,1)S(1)}, bf16[1,512,512]{2,1,0:T(8,128)(2,1)S(1)}, u32[]{:S(2)}, u32[]{:S(2)}) collective-permute-start(bf16[1,512,512]{2,1,0:T(8,128)(2,1)S(1)} %get-tuple-element.75), channel_id=1, source_target_pairs={{0,2},{2,0},{4,6},{6,4},{8,10},{10,8},{12,14},{14,12},{16,18},{18,... | collective-permute-start | bytes 1572872 | tf_op jit(solution)/shard_map/ppermute | solution.py:92
  78.8 46.5 %collective-permute-start.9 = (s32[4,5]{1,0:T(4,128)S(1)}, s32[4,5]{1,0:T(4,128)S(1)}, u32[]{:S(2)}, u32[]{:S(2)}) collective-permute-start(s32[4,5]{1,0:T(4,128)S(1)} %copy-done.15), channel_id=1, source_target_pairs={{0,6},{2,4},{4,2},{6,0},{8,14},{10,12},{12,10},{14,8},{16,22},{18,... | collective-permute-start | bytes 248 | tf_op jit(solution)/shard_map/ppermute | solution.py:92
  79.4 4.9 copy-start.2
  84.3 46.2 %copy-start.16 = (s32[5]{0:T(128)S(1)}, s32[5]{0:T(128)}, u32[]{:S(2)}) copy-start(s32[5]{0:T(128)} %constant.132) | copy-start | bytes 64
  84.7 1.3 copy-start.12
  86.0 1.3 copy-start.14
  125.3 2.8 collective-permute-start.8
  128.1 1.9 collective-permute-start.7
  247.2 14.5 %collective-permute-start.12 = (bf16[1,512,512]{2,1,0:T(8,128)(2,1)S(1)}, bf16[1,512,512]{2,1,0:T(8,128)(2,1)S(1)}, u32[]{:S(2)}, u32[]{:S(2)}) collective-permute-start(bf16[1,512,512]{2,1,0:T(8,128)(2,1)S(1)} %get-tuple-element.71), channel_id=1, source_target_pairs={{0,6},{2,4},{4,2},{6,0},{8,14},{10,12},{12,10},{14,8},{16,22},{18,... | collective-permute-start | bytes 1572872 | tf_op jit(solution)/shard_map/ppermute | solution.py:92
  248.2 24.8 %collective-permute-start.11 = (bf16[1,512,512]{2,1,0:T(8,128)(2,1)S(1)}, bf16[1,512,512]{2,1,0:T(8,128)(2,1)S(1)}, u32[]{:S(2)}, u32[]{:S(2)}) collective-permute-start(bf16[1,512,512]{2,1,0:T(8,128)(2,1)S(1)} %get-tuple-element.72), channel_id=1, source_target_pairs={{0,4},{2,6},{4,0},{6,2},{8,12},{10,14},{12,8},{14,10},{16,20},{18,... | collective-permute-start | bytes 1572872 | tf_op jit(solution)/shard_map/ppermute | solution.py:92
  249.4 23.6 %collective-permute-start.10 = (bf16[1,512,512]{2,1,0:T(8,128)(2,1)S(1)}, bf16[1,512,512]{2,1,0:T(8,128)(2,1)S(1)}, u32[]{:S(2)}, u32[]{:S(2)}) collective-permute-start(bf16[1,512,512]{2,1,0:T(8,128)(2,1)S(1)} %get-tuple-element.73), channel_id=1, source_target_pairs={{0,2},{2,0},{4,6},{6,4},{8,10},{10,8},{12,14},{14,12},{16,18},{18,... | collective-permute-start | bytes 1572872 | tf_op jit(solution)/shard_map/ppermute | solution.py:92
  331.0 14.3 %collective-permute-start.15 = (bf16[512,512]{1,0:T(8,128)(2,1)S(1)}, bf16[512,512]{1,0:T(8,128)(2,1)S(1)}, u32[]{:S(2)}, u32[]{:S(2)}) collective-permute-start(bf16[512,512]{1,0:T(8,128)(2,1)S(1)} %get-tuple-element.67), channel_id=1, source_target_pairs={{0,6},{2,4},{4,2},{6,0},{8,14},{10,12},{12,10},{14,8},{16,22},{18,... | collective-permute-start | bytes 1572872 | tf_op jit(solution)/shard_map/ppermute | solution.py:92
  331.8 24.5 %collective-permute-start.14 = (bf16[512,512]{1,0:T(8,128)(2,1)S(1)}, bf16[512,512]{1,0:T(8,128)(2,1)S(1)}, u32[]{:S(2)}, u32[]{:S(2)}) collective-permute-start(bf16[512,512]{1,0:T(8,128)(2,1)S(1)} %get-tuple-element.68), channel_id=1, source_target_pairs={{0,4},{2,6},{4,0},{6,2},{8,12},{10,14},{12,8},{14,10},{16,20},{18,... | collective-permute-start | bytes 1572872 | tf_op jit(solution)/shard_map/ppermute | solution.py:92
  332.9 23.4 %collective-permute-start.13 = (bf16[512,512]{1,0:T(8,128)(2,1)S(1)}, bf16[512,512]{1,0:T(8,128)(2,1)S(1)}, u32[]{:S(2)}, u32[]{:S(2)}) collective-permute-start(bf16[512,512]{1,0:T(8,128)(2,1)S(1)} %get-tuple-element.69), channel_id=1, source_target_pairs={{0,2},{2,0},{4,6},{6,4},{8,10},{10,8},{12,14},{14,12},{16,18},{18,... | collective-permute-start | bytes 1572872 | tf_op jit(solution)/shard_map/ppermute | solution.py:92
  361.6 12.8 %copy-start.4 = (bf16[512,2048]{1,0:T(8,128)(2,1)S(1)}, bf16[512,2048]{1,0:T(8,128)(2,1)}, u32[]{:S(2)}) copy-start(bf16[512,2048]{1,0:T(8,128)(2,1)} %placed_piece.4) | copy-start | bytes 6291460
  361.6 12.8 %copy-start.13 = (bf16[512,2048]{1,0:T(8,128)(2,1)S(1)}, bf16[512,2048]{1,0:T(8,128)(2,1)}, u32[]{:S(2)}) copy-start(bf16[512,2048]{1,0:T(8,128)(2,1)} %copy-done.12) | copy-start | bytes 6291460
  371.8 13.7 %collective-permute-start.27 = (bf16[2048,2048]{1,0:T(8,128)(2,1)}, bf16[2048,2048]{1,0:T(8,128)(2,1)S(1)}, u32[]{:S(2)}, u32[]{:S(2)}) collective-permute-start(bf16[2048,2048]{1,0:T(8,128)(2,1)} %convolution_convert_fusion), channel_id=1, source_target_pairs={{0,2},{2,0},{4,6},{6,4},{8,10},{10,8},{12,14},{14,12},{16,18},{18,... | collective-permute-start | bytes 25165832 | tf_op jit(solution)/shard_map/ppermute | solution.py:92
  372.5 94.4 %collective-permute-start.20 = (bf16[2,4,512,512]{3,2,1,0:T(8,128)(2,1)}, bf16[2,4,512,512]{3,2,1,0:T(8,128)(2,1)}, u32[]{:S(2)}, u32[]{:S(2)}) collective-permute-start(bf16[2,4,512,512]{3,2,1,0:T(8,128)(2,1)} %get-tuple-element.30), channel_id=1, source_target_pairs={{8,0},{10,2},{12,4},{14,6},{16,8},{18,10},{20,12},{22,14},{24,16},... | collective-permute-start | bytes 12582920 | tf_op jit(solution)/shard_map/ppermute | solution.py:21
  379.5 10.1 %copy-start.1 = (bf16[2048,2048]{1,0:T(8,128)(2,1)}, bf16[2048,2048]{1,0:T(8,128)(2,1)S(1)}, u32[]{:S(2)}) copy-start(bf16[2048,2048]{1,0:T(8,128)(2,1)S(1)} %convolution_convert_fusion.1) | copy-start | bytes 25165828
  385.5 5.3 copy-start
  390.8 92.1 %collective-permute-start.28 = (bf16[2048,1024]{1,0:T(8,128)(2,1)}, bf16[2048,1024]{1,0:T(8,128)(2,1)}, u32[]{:S(2)}, u32[]{:S(2)}) collective-permute-start(bf16[2048,1024]{1,0:T(8,128)(2,1)} %add_convert_fusion), channel_id=1, source_target_pairs={{0,4},{2,6},{4,0},{6,2},{8,12},{10,14},{12,8},{14,10},{16,20},{18,... | collective-permute-start | bytes 12582920 | tf_op jit(solution)/shard_map/ppermute | solution.py:92
  401.1 3.7 copy-start.5
  401.1 108.5 %collective-permute-start.16 = (bf16[512,2048]{1,0:T(8,128)(2,1)}, bf16[512,2048]{1,0:T(8,128)(2,1)}, u32[]{:S(2)}, u32[]{:S(2)}) collective-permute-start(bf16[512,2048]{1,0:T(8,128)(2,1)} %fusion.7), channel_id=1, source_target_pairs={{0,1},{1,0},{2,3},{3,2},{4,5},{5,4},{6,7},{7,6},{8,9},{9,8},{10,11... | collective-permute-start | bytes 6291464 | tf_op jit(solution)/shard_map/ppermute | solution.py:163
  401.1 84.1 %slice-start = ((s8[8388608]{0:T(1024)(128)(4,1)}), s8[4194304]{0:T(1024)(128)(4,1)S(1)}, s32[]{:S(2)}) async-start(s8[8388608]{0:T(1024)(128)(4,1)} %bitcast.111), calls=%async_computation.1 | async-start | bytes 8388608
  401.1 84.1 %slice-start.2 = ((s8[8388608]{0:T(1024)(128)(4,1)}), s8[4194304]{0:T(1024)(128)(4,1)S(1)}, s32[]{:S(2)}) async-start(s8[8388608]{0:T(1024)(128)(4,1)} %bitcast.113), calls=%async_computation.3 | async-start | bytes 8388608
  402.5 93.0 %collective-permute-start.19 = (bf16[512,512]{1,0:T(8,128)(2,1)}, bf16[512,512]{1,0:T(8,128)(2,1)}, u32[]{:S(2)}, u32[]{:S(2)}) collective-permute-start(bf16[512,512]{1,0:T(8,128)(2,1)} %get-tuple-element.63), channel_id=1, source_target_pairs={{0,6},{2,4},{4,2},{6,0},{8,14},{10,12},{12,10},{14,8},{16,22},{18,... | collective-permute-start | bytes 1572872 | tf_op jit(solution)/shard_map/ppermute | solution.py:92
  404.6 80.6 %slice-start.1 = ((s8[8388608]{0:T(1024)(128)(4,1)}), s8[4194304]{0:T(1024)(128)(4,1)S(1)}, s32[]{:S(2)}) async-start(s8[8388608]{0:T(1024)(128)(4,1)} %bitcast.111), calls=%async_computation.2 | async-start | bytes 8388608
  404.6 80.6 %slice-start.3 = ((s8[8388608]{0:T(1024)(128)(4,1)}), s8[4194304]{0:T(1024)(128)(4,1)S(1)}, s32[]{:S(2)}) async-start(s8[8388608]{0:T(1024)(128)(4,1)} %bitcast.113), calls=%async_computation.4 | async-start | bytes 8388608
  404.6 100.8 %collective-permute-start.18 = (bf16[512,512]{1,0:T(8,128)(2,1)}, bf16[512,512]{1,0:T(8,128)(2,1)}, u32[]{:S(2)}, u32[]{:S(2)}) collective-permute-start(bf16[512,512]{1,0:T(8,128)(2,1)} %get-tuple-element.64), channel_id=1, source_target_pairs={{0,4},{2,6},{4,0},{6,2},{8,12},{10,14},{12,8},{14,10},{16,20},{18,... | collective-permute-start | bytes 1572872 | tf_op jit(solution)/shard_map/ppermute | solution.py:92
  466.9 40.5 %collective-permute-start.17 = (bf16[512,512]{1,0:T(8,128)(2,1)}, bf16[512,512]{1,0:T(8,128)(2,1)}, u32[]{:S(2)}, u32[]{:S(2)}) collective-permute-start(bf16[512,512]{1,0:T(8,128)(2,1)} %get-tuple-element.65), channel_id=1, source_target_pairs={{0,2},{2,0},{4,6},{6,4},{8,10},{10,8},{12,14},{14,12},{16,18},{18,... | collective-permute-start | bytes 1572872 | tf_op jit(solution)/shard_map/ppermute | solution.py:92
  482.9 35.3 %collective-permute-start.23 = (bf16[512,512]{1,0:T(8,128)(2,1)S(1)}, bf16[512,512]{1,0:T(8,128)(2,1)S(1)}, u32[]{:S(2)}, u32[]{:S(2)}) collective-permute-start(bf16[512,512]{1,0:T(8,128)(2,1)S(1)} %get-tuple-element.42), channel_id=1, source_target_pairs={{0,6},{2,4},{4,2},{6,0},{8,14},{10,12},{12,10},{14,8},{16,22},{18,... | collective-permute-start | bytes 1572872 | tf_op jit(solution)/shard_map/ppermute | solution.py:92
  495.5 32.4 %collective-permute-start.22 = (bf16[512,512]{1,0:T(8,128)(2,1)S(1)}, bf16[512,512]{1,0:T(8,128)(2,1)S(1)}, u32[]{:S(2)}, u32[]{:S(2)}) collective-permute-start(bf16[512,512]{1,0:T(8,128)(2,1)S(1)} %get-tuple-element.43), channel_id=1, source_target_pairs={{0,4},{2,6},{4,0},{6,2},{8,12},{10,14},{12,8},{14,10},{16,20},{18,... | collective-permute-start | bytes 1572872 | tf_op jit(solution)/shard_map/ppermute | solution.py:92
  505.4 30.7 %collective-permute-start.21 = (bf16[512,512]{1,0:T(8,128)(2,1)}, bf16[512,512]{1,0:T(8,128)(2,1)}, u32[]{:S(2)}, u32[]{:S(2)}) collective-permute-start(bf16[512,512]{1,0:T(8,128)(2,1)} %get-tuple-element.44), channel_id=1, source_target_pairs={{0,2},{2,0},{4,6},{6,4},{8,10},{10,8},{12,14},{14,12},{16,18},{18,... | collective-permute-start | bytes 1572872 | tf_op jit(solution)/shard_map/ppermute | solution.py:92
  507.4 33.3 %collective-permute-start.26 = (bf16[512,512]{1,0:T(8,128)(2,1)}, bf16[512,512]{1,0:T(8,128)(2,1)}, u32[]{:S(2)}, u32[]{:S(2)}) collective-permute-start(bf16[512,512]{1,0:T(8,128)(2,1)} %get-tuple-element.39), channel_id=1, source_target_pairs={{0,6},{2,4},{4,2},{6,0},{8,14},{10,12},{12,10},{14,8},{16,22},{18,... | collective-permute-start | bytes 1572872 | tf_op jit(solution)/shard_map/ppermute | solution.py:92
  507.7 21.5 %copy-start.7 = (bf16[1,512,512]{2,1,0:T(8,128)(2,1)S(1)}, bf16[1,512,512]{2,1,0:T(8,128)(2,1)}, u32[]{:S(2)}) copy-start(bf16[1,512,512]{2,1,0:T(8,128)(2,1)} %get-tuple-element.62) | copy-start | bytes 1572868
  509.6 48.0 %collective-permute-start.31 = (bf16[2048,256]{1,0:T(8,128)(2,1)}, bf16[2048,256]{1,0:T(8,128)(2,1)}, u32[]{:S(2)}, u32[]{:S(2)}) collective-permute-start(bf16[2048,256]{1,0:T(8,128)(2,1)} %get-tuple-element.36), channel_id=1, source_target_pairs={{0,24},{2,26},{4,28},{6,30},{8,0},{10,2},{12,4},{14,6},{16,8},{18,... | collective-permute-start | bytes 3145736 | tf_op jit(solution)/shard_map/ppermute | solution.py:141
  518.2 10.9 %copy-start.8 = (bf16[512,512]{1,0:T(8,128)(2,1)}, bf16[512,512]{1,0:T(8,128)(2,1)S(1)}, u32[]{:S(2)}) copy-start(bf16[512,512]{1,0:T(8,128)(2,1)S(1)} %collective-permute-done.23) | copy-start | bytes 1572868
  518.2 62.7 %collective-permute-start.30 = (bf16[2048,256]{1,0:T(8,128)(2,1)}, bf16[2048,256]{1,0:T(8,128)(2,1)}, u32[]{:S(2)}, u32[]{:S(2)}) collective-permute-start(bf16[2048,256]{1,0:T(8,128)(2,1)} %get-tuple-element.37), channel_id=1, source_target_pairs={{0,16},{2,18},{4,20},{6,22},{8,24},{10,26},{12,28},{14,30},{16,0},... | collective-permute-start | bytes 3145736 | tf_op jit(solution)/shard_map/ppermute | solution.py:141
  527.9 1.3 copy-start.10
  527.9 75.5 %collective-permute-start.29 = (bf16[2048,256]{1,0:T(8,128)(2,1)}, bf16[2048,256]{1,0:T(8,128)(2,1)}, u32[]{:S(2)}, u32[]{:S(2)}) collective-permute-start(bf16[2048,256]{1,0:T(8,128)(2,1)} %get-tuple-element.35), channel_id=1, source_target_pairs={{0,8},{2,10},{4,12},{6,14},{8,16},{10,18},{12,20},{14,22},{16,24},... | collective-permute-start | bytes 3145736 | tf_op jit(solution)/shard_map/ppermute | solution.py:141
  532.1 8.6 %copy-start.3 = (bf16[512,2048]{1,0:T(8,128)(2,1)S(1)}, bf16[512,2048]{1,0:T(8,128)(2,1)}, u32[]{:S(2)}) copy-start(bf16[512,2048]{1,0:T(8,128)(2,1)} %fusion.4) | copy-start | bytes 6291460
  536.0 14.8 %collective-permute-start.25 = (bf16[512,512]{1,0:T(8,128)(2,1)}, bf16[512,512]{1,0:T(8,128)(2,1)}, u32[]{:S(2)}, u32[]{:S(2)}) collective-permute-start(bf16[512,512]{1,0:T(8,128)(2,1)} %get-tuple-element.40), channel_id=1, source_target_pairs={{0,4},{2,6},{4,0},{6,2},{8,12},{10,14},{12,8},{14,10},{16,20},{18,... | collective-permute-start | bytes 1572872 | tf_op jit(solution)/shard_map/ppermute | solution.py:92
  540.7 3.8 copy-start.9
  540.7 3.8 copy-start.11
  540.7 10.2 %collective-permute-start.24 = (bf16[512,512]{1,0:T(8,128)(2,1)}, bf16[512,512]{1,0:T(8,128)(2,1)}, u32[]{:S(2)}, u32[]{:S(2)}) collective-permute-start(bf16[512,512]{1,0:T(8,128)(2,1)} %get-tuple-element.41), channel_id=1, source_target_pairs={{0,2},{2,0},{4,6},{6,4},{8,10},{10,8},{12,14},{14,12},{16,18},{18,... | collective-permute-start | bytes 1572872 | tf_op jit(solution)/shard_map/ppermute | solution.py:92
Sparse Core Ops, SparseCore 0:
  10.2 205.5 all-gather.1
